TPU v7x, 512 devices: a whole 4x4x16 slice. The times are simulated.
512 devices in a mesh: patch: 32 (over y_lo, z), head: 16 (over y_hi, x, core).
Axes of the slice: x: 4, y: 4 (y_hi: 2, y_lo: 2; y = y_hi * 2 + y_lo), z: 16, core: 2. Of those that a mesh axis runs over, the one named last changes fastest.
Arguments:
- state: float32 [4096, 3072], P('patch', 'head'), may hold values from -6 to 6
- mod_weight: bfloat16 [256, 2, 3072], P(None, None, 'head'), may hold values from -0.375 to 0.375
- w_qkv: bfloat16 [3072, 16, 384], P('patch', 'head'), may hold values from -0.109375 to 0.109375
- q_gain: float32 [16, 128], P('head'), as said below
- k_gain: float32 [16, 128], P('head'), may hold values from 1 to 4
- w_in: bfloat16 [3072, 6144], P('patch', 'head'), may hold values from -0.109375 to 0.109375
- w_attn: bfloat16 [2048, 3072], P('head', 'patch'), may hold values from -0.125 to 0.125
- w_out: bfloat16 [6144, 3072], P('head', 'patch'), may hold values from -0.078125 to 0.078125
- cache_keys: bfloat16 [4096, 16, 128], P(None, 'head'), may hold values from -200 to 200
- cache_values: bfloat16 [4096, 16, 128], P(None, 'head'), may hold values from -6 to 6
- timesteps: int32 [4], replicated, may hold values from 0 to 999, as said below
Outputs:
- final_state: float32 [4096, 3072], P('patch', 'head')
Inputs may be any that keep to these rules, and one draw needn't show every extreme that they name: `timesteps`: rises by the same stride from each entry to the next, the stride at least 125; the last entry is 999. `q_gain`: positive.
All inputs are finite; a program needn't handle non-finite values.
Results may differ from a plain program's by a relative error of at most 0.04.
Values may be sent and summed in bfloat16 or wider, within the bound.
A program may use at most 64 MiB of HBM per device.

v0:
```python
import math

import jax
import jax.numpy as jnp
from jax import lax
from jax.sharding import PartitionSpec as P

EMB = 256
SCHED = 1000
STEPS = 3


def sigma_of(index):
    unit = 1.0 - index.astype(jnp.float32) / SCHED
    return 3.0 * unit / (1.0 + 2.0 * unit)


def embed(level):
    half = EMB // 2
    freq = jnp.exp(-math.log(10000.0) * jnp.arange(half, dtype=jnp.float32) / half)
    angle = 1000.0 * level * freq
    return jnp.concatenate([jnp.cos(angle), jnp.sin(angle)]).astype(jnp.bfloat16)


def rms_scale(values, gain):
    return values * lax.rsqrt(jnp.mean(values * values, -1, keepdims=True) + 1e-06) * gain


def on_device(
    state,
    mod_weight,
    w_qkv,
    q_gain,
    k_gain,
    w_in,
    w_attn,
    w_out,
    cache_keys,
    cache_values,
    timesteps,
):
    tok_rows, local_width = state.shape
    heads_here = cache_keys.shape[1]
    head_size = cache_keys.shape[2]
    qkv_rows, in_rows = (
        lax.all_gather(w_qkv, "patch", axis=0, tiled=True),
        lax.all_gather(w_in, "patch", axis=0, tiled=True),
    )
    attn_cols, out_cols = (
        lax.all_gather(w_attn, "patch", axis=1, tiled=True),
        lax.all_gather(w_out, "patch", axis=1, tiled=True),
    )
    qkv_flat = qkv_rows.reshape(qkv_rows.shape[0], heads_here * 3 * head_size)
    start = lax.axis_index("patch") * tok_rows
    keys_cache = cache_keys
    values_cache = cache_values
    x = state
    for step in range(STEPS):
        level_a = sigma_of(timesteps[step])
        level_b = sigma_of(timesteps[step + 1])
        emb = embed(level_a)
        mod_local = jnp.dot(
            emb[None, :],
            mod_weight.reshape(EMB, 2 * local_width),
            preferred_element_type=jnp.float32,
        ).reshape(2, local_width)
        full_rows, full_mod = (
            lax.all_gather(x, "head", axis=1, tiled=True),
            lax.all_gather(mod_local, "head", axis=1, tiled=True),
        )
        mean = jnp.mean(full_rows, -1, keepdims=True)
        var = jnp.mean((full_rows - mean) ** 2, -1, keepdims=True)
        h = (
            (full_rows - mean) * lax.rsqrt(var + 1e-06) * (1.0 + full_mod[0]) + full_mod[1]
        ).astype(jnp.bfloat16)
        qkv = jnp.dot(h, qkv_flat, preferred_element_type=jnp.float32).reshape(
            tok_rows, heads_here, 3 * head_size
        )
        query = rms_scale(qkv[..., :head_size], q_gain).astype(jnp.bfloat16)
        key_new = rms_scale(qkv[..., head_size : 2 * head_size], k_gain).astype(jnp.bfloat16)
        value_new = qkv[..., 2 * head_size :].astype(jnp.bfloat16)
        keys = lax.dynamic_update_slice_in_dim(keys_cache, key_new, start, 0)
        values = lax.dynamic_update_slice_in_dim(values_cache, value_new, start, 0)
        scores = jnp.einsum(
            "qhd,khd->hqk", query, keys, preferred_element_type=jnp.float32
        ) / math.sqrt(head_size)
        prob = jax.nn.softmax(scores, axis=-1).astype(jnp.bfloat16)
        attended = jnp.einsum(
            "hqk,khd->qhd", prob, values, preferred_element_type=jnp.float32
        ).astype(jnp.bfloat16)
        attended = attended.reshape(tok_rows, heads_here * head_size)
        hidden = jax.nn.gelu(
            jnp.dot(h, in_rows, preferred_element_type=jnp.float32), approximate=True
        ).astype(jnp.bfloat16)
        term = jnp.dot(attended, attn_cols, preferred_element_type=jnp.float32) + jnp.dot(
            hidden, out_cols, preferred_element_type=jnp.float32
        )
        summed = lax.psum(term.astype(jnp.bfloat16), "head").astype(jnp.float32)
        velocity = lax.dynamic_slice_in_dim(
            summed, lax.axis_index("head") * local_width, local_width, 1
        )
        if step < STEPS - 1:
            own_keys = lax.dynamic_slice_in_dim(keys_cache, start, tok_rows, 0)
            own_values = lax.dynamic_slice_in_dim(values_cache, start, tok_rows, 0)
            delta_keys = (key_new.astype(jnp.float32) - own_keys.astype(jnp.float32)).astype(
                jnp.bfloat16
            )
            delta_values = (value_new.astype(jnp.float32) - own_values.astype(jnp.float32)).astype(
                jnp.bfloat16
            )
            all_keys, all_values = (
                lax.all_gather(delta_keys, "patch", axis=0, tiled=True),
                lax.all_gather(delta_values, "patch", axis=0, tiled=True),
            )
            keys_cache = (keys_cache.astype(jnp.float32) + all_keys.astype(jnp.float32)).astype(
                jnp.bfloat16
            )
            values_cache = (
                values_cache.astype(jnp.float32) + all_values.astype(jnp.float32)
            ).astype(jnp.bfloat16)
        x = x + (level_b - level_a) * velocity
    return x


def solution(mesh):
    in_specs = (
        P("patch", "head"),
        P(None, None, "head"),
        P("patch", "head", None),
        P("head", None),
        P("head", None),
        P("patch", "head"),
        P("head", "patch"),
        P("head", "patch"),
        P(None, "head", None),
        P(None, "head", None),
        P(),
    )
    out_specs = P("patch", "head")
    return jax.shard_map(
        on_device, mesh=mesh, in_specs=in_specs, out_specs=out_specs, check_vma=False
    )
```

profile of v0, /device:TPU:1, one launch (start us, length us, event | category | flops | bytes accessed | tf_op | source)
XLA Modules:
  0.0 1620.5 jit_solution(9888186613113917359)
XLA Ops:
  6.5 1.3 copy.35
  7.9 0.2 copy-done.14
  8.1 1.0 copy.36
  9.2 0.7 all-gather.16.cloned.1.call-update
  10.0 0.7 all-gather.20.cloned.1.call-update
  10.7 0.5 all-gather.18.cloned.1.call-update
  11.3 0.7 fusion.111
  12.9 25.7 %all-gather = f32[16,192,2]{1,2,0:T(2,128)S(1)} all-gather(f32[1,192,2]{1,2,0:T(2,128)S(1)} %bitcast.179), channel_id=1, replica_groups=mesh['patch'=32,'head'=16] {'head'}, dimensions={0}, use_global_device_ids=true | all-gather | bytes 26112 | tf_op jit(solution)/shard_map/all_gather | solution.py:69
  38.8 39.8 %all-gather.14.cloned.1.call-done = f32[128,3072]{0,1:T(8,128)} async-done(((f32[128,192]{0,1:T(8,128)}), f32[128,3072]{0,1:T(8,128)}) %all-gather.14.cloned.1.call-update) | async-done | bytes 1572880 | tf_op jit(solution)/shard_map/all_gather | solution.py:68
  78.6 1.9 reduce_sum.135
  80.5 0.4 multiply_reduce_fusion.2
  81.0 111.9 %all-gather.16.cloned.1.call-done = bf16[3072,1,384]{2,0,1:T(8,128)(2,1)} async-done(((bf16[96,1,384]{2,0,1:T(8,128)(2,1)}), bf16[3072,1,384]{2,0,1:T(8,128)(2,1)}) %all-gather.16.cloned.1.call-update) | async-done | bytes 2359312 | tf_op jit(solution)/shard_map/all_gather | solution.py:46
  192.9 3.8 fusion.12
  196.9 1.5 subtract_convert_fusion.2
  198.4 0.5 all-gather.26.cloned.1.call-update
  199.0 58.8 %all_gather.45 = bf16[128,3072]{0,1:T(8,128)(2,1)} all-gather(bf16[128,96]{0,1:T(8,128)(2,1)S(1)} %copy-done.18), channel_id=1, replica_groups=mesh['patch'=32,'head'=16] {'patch'}, dimensions={1}, use_global_device_ids=true | all-gather | bytes 811008 | tf_op jit(solution)/shard_map/all_gather | solution.py:50
  257.8 65.9 %all-gather.20.cloned.1.call-done = bf16[384,3072]{0,1:T(8,128)(2,1)} async-done(((bf16[384,96]{0,1:T(8,128)(2,1)}), bf16[384,3072]{0,1:T(8,128)(2,1)}) %all-gather.20.cloned.1.call-update) | async-done | bytes 2359312 | tf_op jit(solution)/shard_map/all_gather | solution.py:51
  323.7 128.3 %all-gather.18.cloned.1.call-done = bf16[3072,384]{1,0:T(8,128)(2,1)} async-done(((bf16[96,384]{1,0:T(8,128)(2,1)}), bf16[3072,384]{1,0:T(8,128)(2,1)}) %all-gather.18.cloned.1.call-update) | async-done | bytes 2359312 | tf_op jit(solution)/shard_map/all_gather | solution.py:47
  452.1 6.0 fusion.66
  458.1 119.7 %all-gather.22.cloned.1.call-done = bf16[4096,1,128]{2,0,1:T(8,128)(2,1)} async-done(((bf16[128,1,128]{2,0,1:T(8,128)(2,1)}), bf16[4096,1,128]{2,0,1:T(8,128)(2,1)}) %all-gather.22.cloned.1.call-update) | async-done | bytes 1048592 | tf_op jit(solution)/shard_map/all_gather | solution.py:113
  577.8 2.5 add_convert_fusion.3
  580.3 124.2 %all-gather.26.cloned.1.call-done = bf16[4096,1,128]{2,0,1:T(8,128)(2,1)} async-done(((bf16[128,1,128]{2,0,1:T(8,128)(2,1)}), bf16[4096,1,128]{2,0,1:T(8,128)(2,1)}) %all-gather.26.cloned.1.call-update) | async-done | bytes 1048592 | tf_op jit(solution)/shard_map/all_gather | solution.py:112
  704.5 1.5 add_convert_fusion.2
  706.0 0.6 bitcast_dynamic-update-slice_fusion.2
  706.6 0.6 fusion.112
  707.2 1.4 copy-done.7
  708.6 0.4 fusion.9
  709.0 0.2 copy-done.11
  709.2 4.4 fusion
  714.4 168.7 %all-reduce.4.cloned.1.call-done = bf16[128,3072]{0,1:T(8,128)(2,1)} async-done(((bf16[128,3072]{0,1:T(8,128)(2,1)}), bf16[128,3072]{0,1:T(8,128)(2,1)}) %all-reduce.4.cloned.1.call-update) | async-done | bytes 786448 | tf_op jit(solution)/shard_map/psum | solution.py:98
  883.2 1.5 multiply_add_fusion.2
  884.9 21.1 %all-gather.1 = f32[16,192,2]{1,2,0:T(2,128)S(1)} all-gather(f32[1,192,2]{1,2,0:T(2,128)S(1)} %bitcast.180), channel_id=1, replica_groups=mesh['patch'=32,'head'=16] {'head'}, dimensions={0}, use_global_device_ids=true | all-gather | bytes 26112 | tf_op jit(solution)/shard_map/all_gather | solution.py:69
  906.2 44.7 %all-gather.24.cloned.1.call-done = f32[128,3072]{0,1:T(8,128)} async-done(((f32[128,192]{0,1:T(8,128)}), f32[128,3072]{0,1:T(8,128)}) %all-gather.24.cloned.1.call-update) | async-done | bytes 1572880 | tf_op jit(solution)/shard_map/all_gather | solution.py:68
  950.8 1.9 reduce_sum.140
  952.8 0.4 multiply_reduce_fusion.1
  953.2 3.8 fusion.15
  957.1 1.5 subtract_convert_fusion
  958.7 0.5 all-gather.32.cloned.1.call-update
  959.2 0.2 all-reduce.6.cloned.1.call-start
  959.5 6.0 fusion.64
  965.5 101.9 %all-gather.28.cloned.1.call-done = bf16[4096,1,128]{2,0,1:T(8,128)(2,1)} async-done(((bf16[128,1,128]{2,0,1:T(8,128)(2,1)}), bf16[4096,1,128]{2,0,1:T(8,128)(2,1)}) %all-gather.28.cloned.1.call-update) | async-done | bytes 1048592 | tf_op jit(solution)/shard_map/all_gather | solution.py:113
  1067.3 2.8 fusion.24
  1070.2 124.1 %all-gather.32.cloned.1.call-done = bf16[4096,1,128]{2,0,1:T(8,128)(2,1)} async-done(((bf16[128,1,128]{2,0,1:T(8,128)(2,1)}), bf16[4096,1,128]{2,0,1:T(8,128)(2,1)}) %all-gather.32.cloned.1.call-update) | async-done | bytes 1048592 | tf_op jit(solution)/shard_map/all_gather | solution.py:112
  1194.2 2.5 fusion.25
  1196.8 0.6 fusion.113
  1197.4 1.4 copy-done.8
  1198.8 0.4 fusion.10
  1199.2 0.3 copy-done.13
  1199.6 4.0 fusion.1
  1204.3 169.0 %all-reduce.6.cloned.1.call-done = bf16[128,3072]{0,1:T(8,128)(2,1)} async-done(((bf16[128,3072]{0,1:T(8,128)(2,1)}), bf16[128,3072]{0,1:T(8,128)(2,1)}) %all-reduce.6.cloned.1.call-update) | async-done | bytes 786448 | tf_op jit(solution)/shard_map/psum | solution.py:98
  1373.3 1.5 multiply_add_fusion.1
  1375.1 21.1 %all-gather.2 = f32[16,192,2]{1,2,0:T(2,128)S(1)} all-gather(f32[1,192,2]{1,2,0:T(2,128)S(1)} %bitcast.181), channel_id=1, replica_groups=mesh['patch'=32,'head'=16] {'head'}, dimensions={0}, use_global_device_ids=true | all-gather | bytes 26112 | tf_op jit(solution)/shard_map/all_gather | solution.py:69
  1396.3 44.0 %all-gather.30.cloned.1.call-done = f32[128,3072]{0,1:T(8,128)} async-done(((f32[128,192]{0,1:T(8,128)}), f32[128,3072]{0,1:T(8,128)}) %all-gather.30.cloned.1.call-update) | async-done | bytes 1572880 | tf_op jit(solution)/shard_map/all_gather | solution.py:68
  1440.3 1.9 reduce_sum.145
  1442.3 0.4 multiply_reduce_fusion
  1442.7 3.9 fusion.18
  1446.8 0.6 fusion.87
  1447.4 0.6 fusion.114
  1448.0 1.4 copy-done.6
  1449.3 0.4 fusion.11
  1449.8 4.8 fusion.62
  1454.6 4.3 fusion.2
  1459.6 152.9 %all-reduce.8.cloned.1.call-done = bf16[128,3072]{0,1:T(8,128)(2,1)} async-done(((bf16[128,3072]{0,1:T(8,128)(2,1)}), bf16[128,3072]{0,1:T(8,128)(2,1)}) %all-reduce.8.cloned.1.call-update) | async-done | bytes 786448 | tf_op jit(solution)/shard_map/psum | solution.py:98
  1612.5 1.5 multiply_add_fusion
  (98 shorter events, 2.1 us)
Async XLA Ops:
  6.5 6.2 copy-start
  6.5 1.6 copy-start.14
  6.5 4.8 copy-start.20
  6.5 72.0 %all-gather.14.cloned.1.call-start = ((), (), s32[]{:S(2)}) async-start(), calls=%async_computation | async-start | bytes 1671168 | tf_op jit(solution)/shard_map/all_gather | solution.py:68
  8.1 188.7 %copy-start.4 = (bf16[4096,1,128]{2,0,1:T(8,128)(2,1)}, bf16[4096,1,128]{2,0,1:T(8,128)(2,1)S(1)}, u32[]{:S(2)}) copy-start(bf16[4096,1,128]{2,0,1:T(8,128)(2,1)S(1)} %copy.35) | copy-start | bytes 3145732
  9.2 183.7 %all-gather.16.cloned.1.call-start = ((), (), s32[]{:S(2)}) async-start(), calls=%async_computation.1 | async-start | bytes 2433024 | tf_op jit(solution)/shard_map/all_gather | solution.py:46
  9.9 313.8 %all-gather.20.cloned.1.call-start = ((), (), s32[]{:S(2)}) async-start(), calls=%async_computation.3 | async-start | bytes 2433024 | tf_op jit(solution)/shard_map/all_gather | solution.py:51
  10.7 441.4 %all-gather.18.cloned.1.call-start = ((), (), s32[]{:S(2)}) async-start(), calls=%async_computation.2 | async-start | bytes 2433024 | tf_op jit(solution)/shard_map/all_gather | solution.py:47
  11.2 566.6 %all-gather.22.cloned.1.call-start = ((), (), s32[]{:S(2)}) async-start(), calls=%async_computation.5 | async-start | bytes 1081344 | tf_op jit(solution)/shard_map/all_gather | solution.py:113
  78.6 2.0 copy-start.1
  192.9 4.0 copy-start.19
  192.9 6.1 copy-start.18
  198.4 506.1 %all-gather.26.cloned.1.call-start = ((), (), s32[]{:S(2)}) async-start(), calls=%async_computation.7 | async-start | bytes 1081344 | tf_op jit(solution)/shard_map/all_gather | solution.py:112
  198.9 684.2 %all-reduce.4.cloned.1.call-start = ((), (), s32[]{:S(2)}) async-start(), calls=%async_computation.4 | async-start | bytes 1572864 | tf_op jit(solution)/shard_map/psum | solution.py:98
  257.8 320.0 %copy-start.10 = (bf16[4096,1,128]{2,0,1:T(8,128)(2,1)S(1)}, bf16[4096,1,128]{2,0,1:T(8,128)(2,1)}, u32[]{:S(2)}) copy-start(bf16[4096,1,128]{2,0,1:T(8,128)(2,1)} %copy.36) | copy-start | bytes 3145732
  458.1 246.4 %copy-start.5 = (bf16[4096,1,128]{2,0,1:T(8,128)(2,1)S(1)}, bf16[4096,1,128]{2,0,1:T(8,128)(2,1)}, u32[]{:S(2)}) copy-start(bf16[4096,1,128]{2,0,1:T(8,128)(2,1)} %copy-done.4) | copy-start | bytes 3145732
  580.3 126.3 %copy-start.21 = (f32[1,128]{1,0:T(1,128)S(1)}, f32[1,128]{1,0:T(1,128)}, u32[]{:S(2)}) copy-start(f32[1,128]{1,0:T(1,128)} %param.14) | copy-start | bytes 1540
  707.2 1.4 copy-start.7
  707.2 2.0 copy-start.11
  709.2 174.0 %copy-start.17 = (f32[128,192]{0,1:T(8,128)S(1)}, f32[128,192]{0,1:T(8,128)}, u32[]{:S(2)}) copy-start(f32[128,192]{0,1:T(8,128)} %param.11) | copy-start | bytes 294916
  713.6 237.2 %all-gather.24.cloned.1.call-start = ((), (), s32[]{:S(2)}) async-start(), calls=%async_computation.6 | async-start | bytes 1671168 | tf_op jit(solution)/shard_map/all_gather | solution.py:68
  884.6 182.7 %all-gather.28.cloned.1.call-start = ((), (), s32[]{:S(2)}) async-start(), calls=%async_computation.9 | async-start | bytes 1081344 | tf_op jit(solution)/shard_map/all_gather | solution.py:113
  950.8 2.0 copy-start.2
  958.6 235.6 %all-gather.32.cloned.1.call-start = ((), (), s32[]{:S(2)}) async-start(), calls=%async_computation.11 | async-start | bytes 1081344 | tf_op jit(solution)/shard_map/all_gather | solution.py:112
  959.2 414.1 %all-reduce.6.cloned.1.call-start = ((), (), s32[]{:S(2)}) async-start(), calls=%async_computation.8 | async-start | bytes 1572864 | tf_op jit(solution)/shard_map/psum | solution.py:98
  1070.2 126.5 %copy-start.9 = (bf16[4096,1,128]{2,0,1:T(8,128)(2,1)S(1)}, bf16[4096,1,128]{2,0,1:T(8,128)(2,1)}, u32[]{:S(2)}) copy-start(bf16[4096,1,128]{2,0,1:T(8,128)(2,1)} %add_convert_fusion.3) | copy-start | bytes 3145732
  1197.4 1.4 copy-start.8
  1197.4 2.2 copy-start.13
  1199.5 173.8 %copy-start.15 = (f32[128,192]{0,1:T(8,128)S(1)}, f32[128,192]{0,1:T(8,128)}, u32[]{:S(2)}) copy-start(f32[128,192]{0,1:T(8,128)} %multiply_add_fusion.2) | copy-start | bytes 294916
  1203.6 236.7 %all-gather.30.cloned.1.call-start = ((), (), s32[]{:S(2)}) async-start(), calls=%async_computation.10 | async-start | bytes 1671168 | tf_op jit(solution)/shard_map/all_gather | solution.py:68
  1374.8 237.7 %all-reduce.8.cloned.1.call-start = ((), (), s32[]{:S(2)}) async-start(), calls=%async_computation.12 | async-start | bytes 1572864 | tf_op jit(solution)/shard_map/psum | solution.py:98
  1440.3 2.0 copy-start.3
  1442.7 4.0 copy-start.12
  1447.9 1.4 copy-start.6
  1454.6 157.9 %copy-start.16 = (f32[128,192]{0,1:T(8,128)S(1)}, f32[128,192]{0,1:T(8,128)}, u32[]{:S(2)}) copy-start(f32[128,192]{0,1:T(8,128)} %multiply_add_fusion.1) | copy-start | bytes 294916
Sparse Core Ops, SparseCore 0:
  10.7 67.8 all-gather.13
  80.6 112.2 all-gather.15
  195.0 128.7 all-gather.19
  325.7 126.3 all-gather.17
  454.0 123.7 all-gather.21
  579.7 124.7 all-gather.25
  713.8 169.3 all-reduce.3
  887.0 63.7 all-gather.23
  958.7 108.5 all-gather.27
  1069.5 124.7 all-gather.31
  1203.7 169.5 all-reduce.5
  1376.5 63.7 all-gather.29
  1459.1 153.3 all-reduce.7
where the time goes:
time: 1620 us
  waiting for transfers between devices  1400 us (86%)
  blocking collectives  127 us (8%)
  matrix products  43.3 us (3%)
  other arithmetic  27 us (2%)
  between operations  16.3 us (1%)
    psum x3, waiting for transfers between devices, on_device(): summed = lax.psum(term.astype(jnp.bfloat16), 'head').astype(jnp.float32)  491 us
    all_gather x2, waiting for transfers between devices, on_device(): lax.all_gather(delta_keys, 'patch', axis=0, tiled=True)  248 us
    all_gather x2, waiting for transfers between devices, on_device(): lax.all_gather(delta_values, 'patch', axis=0, tiled=True)  222 us
    all_gather x3, waiting for transfers between devices, on_device(): lax.all_gather(x, 'head', axis=1, tiled=True)  128 us
    all_gather x1, waiting for transfers between devices, on_device(): lax.all_gather(w_in, 'patch', axis=0, tiled=True)  128 us
    all_gather x1, waiting for transfers between devices, on_device(): lax.all_gather(w_qkv, 'patch', axis=0, tiled=True)  112 us
    all_gather x3, blocking collectives, on_device(): lax.all_gather(mod_local, 'head', axis=1, tiled=True)  68 us
    all_gather x1, waiting for transfers between devices, on_device(): lax.all_gather(w_out, 'patch', axis=1, tiled=True)  65.9 us
  transfers between devices with their start and end apart: 13, of which 13 were waited for; matrix products, arithmetic and copies ran while one was open for 2% of the time, Pallas kernels for 0%

commit v1 on v0

v1 whole, which is shorter than its diff:
```python
import math

import jax
import jax.numpy as jnp
from jax import lax
from jax.experimental import pallas as pl
from jax.experimental.pallas import tpu as pltpu
from jax.sharding import PartitionSpec as P

MESH = pl.DeviceIdType.MESH
F32 = jnp.float32
BF16 = jnp.bfloat16
SCHED = 1000
STEPS = 3
Z = 16
CHIPS = 16
TOK = 128
D = 3072
HALF = D // 2
HD = 128
ROWS = 96
KEYS = 4096
CHUNK = 512
NT = (((1,), (1,)), ((), ()))


def sigma(unit_index):
    unit = 1.0 - unit_index / SCHED
    return 3.0 * unit / (1.0 + 2.0 * unit)


def kernel(
    times, state, mod_w, w_qkv, w_in, w_attn, w_out, q_gain, k_gain, cache_k, cache_v,
    out,
    wq, wi, wo, kv, hland, rland, tsend, hb, og, scores, xs, xl, fs, fl, xt, mw, modp, xp, gains,
    cache_s, cache_r, swap_s, swap_r, ring_s, ring_r, pair_s, pair_r,
    kring_s, kring_r, kpair_s, kpair_r, x_s, x_r, ag_s, ag_r, rs_s, rs_r, f_s, f_r, local,
):
    patch = lax.axis_index("patch")
    head = lax.axis_index("head")
    yl, z = lax.div(patch, Z), lax.rem(patch, Z)
    yh, x, c = lax.div(head, 8), lax.rem(lax.div(head, 2), 4), lax.rem(head, 2)
    y = yh * 2 + yl
    me = y * 4 + x
    own = c * Z + z
    natural = c == yl

    def dev(yy, xx, cc, zz):
        return (lax.rem(yy, 2) * Z + zz, lax.div(yy, 2) * 8 + xx * 2 + cc)

    def chip_at(o):
        return lax.rem(y + lax.div(o, 4), 4), lax.rem(x + lax.rem(o, 4), 4)

    def chip_from(o):
        return lax.rem(y + 4 - lax.div(o, 4), 4), lax.rem(x + 4 - lax.rem(o, 4), 4)

    def remote(src, dst, send, recv, device):
        return pltpu.make_async_remote_copy(
            src_ref=src, dst_ref=dst, send_sem=send, recv_sem=recv, device_id=device, device_id_type=MESH
        )

    partner = dev(y, x, 1 - c, z)
    z_next = (dev(y, x, c, lax.rem(z + 1, Z)), dev(y, x, c, lax.rem(z + Z - 1, Z)))
    twin = dev(yh * 2 + c, x, yl, z)

    barrier = pltpu.get_barrier_semaphore()

    def greet(device):
        pl.semaphore_signal(barrier, inc=1, device_id=device, device_id_type=MESH)

    def greet_chip(o, carry):
        yy, xx = chip_at(o)
        greet(dev(yy, xx, c, z))
        greet(dev(yy, xx, 1 - c, z))
        return carry

    greet(z_next[0])
    greet(z_next[1])
    greet(partner)
    lax.fori_loop(1, CHIPS, greet_chip, 0)

    weights = (wq, wi, wo)

    def slab(j, zz, part=None):
        start, size = (c * Z + zz) * ROWS, ROWS
        if part is not None:
            start, size = start + part * (ROWS // 2), ROWS // 2
        return weights[j].at[pl.ds(pl.multiple_of(start, 16), size), :]

    def shard_parts():
        base = pl.ds(pl.multiple_of(own * ROWS, 16), ROWS)
        swapped = pl.ds(pl.multiple_of((yl * Z + z) * ROWS, 16), ROWS)
        return (
            (w_qkv, wq.at[base, :], wq.at[swapped, :]),
            (w_in, wi.at[base, :], wi.at[swapped, :]),
            (w_attn, wo.at[base, 0:HD], wo.at[swapped, 0:HD]),
            (w_out, wo.at[base, HD:512], wo.at[swapped, HD:512]),
        )

    def caches():
        return (
            (cache_k, kv.at[0, 0]),
            (cache_v, kv.at[0, 1]),
            (q_gain, gains.at[0]),
            (k_gain, gains.at[1]),
        )

    pl.semaphore_wait(barrier, 33)

    for i, (src, here, there) in enumerate(shard_parts()):
        @pl.when(natural)
        def _():
            pltpu.make_async_copy(src, here, swap_r.at[i]).start()

        @pl.when(jnp.logical_not(natural))
        def _():
            remote(src, there, swap_s.at[i], swap_r.at[i], twin).start()

    @pl.when(natural)
    def _():
        for i, (src, dst) in enumerate(caches()):
            pltpu.make_async_copy(src, dst, local.at[i]).start()
            remote(src, dst, cache_s.at[i], cache_r.at[i], partner).start()

    def wait_own(i):
        src, here, there = shard_parts()[i]
        pltpu.make_async_copy(src, here, swap_r.at[i]).wait()

    def pair_copy(j, zz):
        part = slab(j, zz)
        return remote(part, part, pair_s.at[j, zz], pair_r.at[j, zz], partner)

    def pair_wait(j, zz):
        start = pl.multiple_of(((1 - c) * Z + zz) * ROWS, 16)
        part = weights[j].at[pl.ds(start, ROWS), :]
        remote(part, part, pair_s.at[j, zz], pair_r.at[j, zz], partner).wait_recv()

    def ring_copy(j, d, k, zz, part=None):
        block = slab(j, zz, part)
        return remote(block, block, ring_s.at[j, d, k], ring_r.at[j, d, k], z_next[d])

    def source(d, k):
        return lax.rem(z + Z - k, Z) if d == 0 else lax.rem(z + k, Z)

    def ring_start():
        for j in range(3):
            wait_own(j)
            if j == 2:
                wait_own(3)
            for d in range(2):
                ring_copy(j, d, 0, z).start()
            pair_copy(j, z).start()

    def ring_hop(k, last=False):
        for j in range(3):
            for d in range(2):
                zz = source(d, k)
                ring_copy(j, d, k - 1, zz).wait_recv()
                ring_copy(j, d, k, zz, d if last else None).start()
                pair_copy(j, zz).start()

    def ring_end():
        zz = source(0, 8)
        for j in range(3):
            for d in range(2):
                ring_copy(j, d, 7, zz, d).wait_recv()
            pair_copy(j, zz).start()

    ring_start()

    row = lax.broadcasted_iota(jnp.int32, (8, HD), 0)
    lane = lax.broadcasted_iota(jnp.int32, (8, HD), 1)
    stepped = lax.rem(row, 3)
    when = jnp.zeros((8, HD), F32)
    for s in range(STEPS):
        when = jnp.where(stepped == s, times[s].astype(F32), when)
    freq = jnp.exp(-math.log(10000.0) * lane.astype(F32) / HD)
    angle = 1000.0 * sigma(when) * freq
    emb = jnp.concatenate([jnp.cos(angle), jnp.sin(angle)], axis=1).astype(BF16)
    place = pl.ds(pl.multiple_of(c * 64, 64), 192)
    mw[...] = jnp.zeros_like(mw)
    xt[...] = jnp.zeros_like(xt)
    for j in range(2):
        mw[j, place, :] = mod_w[j]
    xt[place, :] = state[...]
    mods = [lax.dot_general(emb, mw[j], NT, preferred_element_type=F32) for j in range(2)]
    row2 = lax.broadcasted_iota(jnp.int32, (8, 256), 0)
    mod_rows = jnp.where(row2 < 3, mods[0], mods[1])
    rows_here = xt[...].T
    for q in range(CHIPS):
        xs[q, 0:8] = rows_here[8 * q : 8 * q + 8]
        xs[q, 8:16] = mod_rows

    def x_copy(q, device):
        return remote(xs.at[q], xl.at[head], x_s.at[q], x_r.at[head], device)

    @pl.when(natural)
    def _():
        pltpu.make_async_copy(xs.at[me], xl.at[head], x_r.at[head]).start()

    @pl.when(jnp.logical_not(natural))
    def _():
        x_copy(me, partner).start()

    def x_start(o, carry):
        yy, xx = chip_at(o)
        x_copy(yy * 4 + xx, dev(yy, xx, yl, z)).start()
        return carry

    lax.fori_loop(1, CHIPS, x_start, 0)

    def loop_hops(lo, hi):
        def body(k, carry):
            ring_hop(k)
            return carry

        lax.fori_loop(lo, hi, body, 0)

    loop_hops(1, 3)

    def x_wait(r, carry):
        remote(xs.at[0], xl.at[r], x_s.at[0], x_r.at[r], partner).wait_recv()
        return carry

    lax.fori_loop(0, CHIPS, x_wait, 0)
    for k in range(8):
        a, b = xl[2 * k], xl[2 * k + 1]
        group = jnp.concatenate([a[:, :HD], a[:, HD:] + b[:, :HD], b[:, HD:]], axis=1)
        rows, cols = slice(8 * (k // 4), 8 * (k // 4) + 8), slice(384 * (k % 4), 384 * (k % 4) + 384)
        xp[rows, cols] = group[0:8]
        for i in range(6):
            modp[i, rows, cols] = jnp.broadcast_to(group[8 + i : 9 + i], (8, 384))

    def fold(sums):
        total = (sums[0:8] + sums[8:16]) * (1.0 / D)
        return jnp.concatenate([total, total], axis=0)

    my_slot = pl.ds(pl.multiple_of(me * 16, 16), 16)

    def slot(yy, xx):
        return pl.ds(pl.multiple_of((yy * 4 + xx) * 16, 16), 16)

    def ag_start(s):
        rows = xp[...]
        delta = rows - fold(jnp.sum(rows, axis=1, keepdims=True))
        var = fold(jnp.sum(delta * delta, axis=1, keepdims=True))
        h = delta * lax.rsqrt(var + 1e-06) * (1.0 + modp[s]) + modp[3 + s]
        hland[s, my_slot, :] = h.astype(BF16)

        def body(o, carry):
            yy, xx = chip_at(o)
            block = hland.at[s, my_slot, :]
            remote(block, block, ag_s.at[s, o], ag_r.at[s, o], dev(yy, xx, c, z)).start()
            return carry

        lax.fori_loop(1, CHIPS, body, 0)

    def ag_wait(s, lo=1, hi=CHIPS):
        def body(o, carry):
            yy, xx = chip_from(o)
            block = hland.at[s, slot(yy, xx), :]
            remote(block, block, ag_s.at[s, o], ag_r.at[s, o], partner).wait_recv()
            return carry

        lax.fori_loop(lo, hi, body, 0)

    def unpack(s):
        for m in range(8):
            block = hland[s, 32 * m : 32 * m + 32, :].astype(F32)
            rows = slice(16 * m, 16 * m + 16)
            hb[rows, 0:HALF] = jnp.concatenate([block[0:8], block[16:24]], axis=0).astype(BF16)
            hb[rows, HALF:D] = jnp.concatenate([block[8:16], block[24:32]], axis=0).astype(BF16)

    ag_start(0)
    loop_hops(3, 7)
    ag_wait(0)
    unpack(0)
    ring_hop(7, last=True)
    ring_end()

    def pair_loop(zz, carry):
        for j in range(3):
            pair_wait(j, zz)
        return carry

    lax.fori_loop(0, Z, pair_loop, 0)

    @pl.when(natural)
    def _():
        for i, (src, dst) in enumerate(caches()):
            pltpu.make_async_copy(src, dst, local.at[i]).wait()
            remote(src, dst, cache_s.at[i], cache_r.at[i], partner).wait_send()

    @pl.when(jnp.logical_not(natural))
    def _():
        for i, (src, dst) in enumerate(caches()):
            remote(src, dst, cache_s.at[i], cache_r.at[i], partner).wait_recv()

    def kv_block(s, cc, zz, part=None):
        start, size = (cc * Z + zz) * TOK, TOK
        if part is not None:
            start, size = start + part * (TOK // 2), TOK // 2
        return kv.at[s + 1, :, pl.ds(pl.multiple_of(start, 16), size), :]

    def kring_copy(s, d, k, zz, part=None):
        block = kv_block(s, c, zz, part)
        return remote(block, block, kring_s.at[s, d, k], kring_r.at[s, d, k], z_next[d])

    def kpair_copy(s, zz):
        block = kv_block(s, c, zz)
        return remote(block, block, kpair_s.at[s, zz], kpair_r.at[s, zz], partner)

    def kv_start(s):
        for d in range(2):
            kring_copy(s, d, 0, z).start()
        kpair_copy(s, z).start()

    def kv_hop(s, k):
        if s >= STEPS - 1:
            return
        if k < 8:
            for d in range(2):
                zz = source(d, k)
                kring_copy(s, d, k - 1, zz).wait_recv()
                kring_copy(s, d, k, zz, d if k == 7 else None).start()
                kpair_copy(s, zz).start()
        else:
            zz = source(0, 8)
            for d in range(2):
                kring_copy(s, d, 7, zz, d).wait_recv()
            kpair_copy(s, zz).start()

    def kv_wait(s):
        def body(zz, carry):
            block = kv_block(s, 1 - c, zz)
            remote(block, block, kpair_s.at[s, zz], kpair_r.at[s, zz], partner).wait_recv()
            return carry

        lax.fori_loop(0, Z, body, 0)

    def kv_sent(s):
        def body(k, carry):
            for d in range(2):
                kring_copy(s, d, k, z).wait_send()
            return carry

        lax.fori_loop(0, 7, body, 0)
        for d in range(2):
            kring_copy(s, d, 7, z, d).wait_send()

        def pairs(zz, carry):
            kpair_copy(s, zz).wait_send()
            return carry

        lax.fori_loop(0, Z, pairs, 0)

    def rms(values, gain):
        return values * lax.rsqrt(jnp.mean(values * values, axis=1, keepdims=True) + 1e-06) * gain

    own_rows = pl.ds(pl.multiple_of(own * TOK, 16), TOK)

    for s in range(STEPS):
        qkv = jnp.dot(hb[...], wq[...], preferred_element_type=F32)
        query = rms(qkv[:, 0:HD], gains[0]).astype(BF16)
        fresh = (rms(qkv[:, HD : 2 * HD], gains[1]).astype(BF16), qkv[:, 2 * HD :].astype(BF16))
        if s > 0:
            kv_sent(s - 1)
        for i in range(2):
            old = kv[s, i, own_rows, :].astype(F32)
            if s < STEPS - 1:
                change = (fresh[i].astype(F32) - old).astype(BF16)
                kv[s + 1, i, own_rows, :] = (old + change.astype(F32)).astype(BF16)
            kv[s, i, own_rows, :] = fresh[i]
        if s < STEPS - 1:
            kv_start(s)
        top = jnp.full((TOK, 1), -jnp.inf, F32)
        for j in range(KEYS // CHUNK):
            cols = slice(CHUNK * j, CHUNK * j + CHUNK)
            score = lax.dot_general(query, kv[s, 0, cols, :], NT, preferred_element_type=F32)
            score = score * (1.0 / math.sqrt(HD))
            scores[:, cols] = score
            top = jnp.maximum(top, jnp.max(score, axis=1, keepdims=True))
        mass = jnp.zeros((TOK, 1), F32)
        mixed = jnp.zeros((TOK, HD), F32)
        for j in range(KEYS // CHUNK):
            cols = slice(CHUNK * j, CHUNK * j + CHUNK)
            weight = jnp.exp(scores[:, cols] - top)
            mass = mass + jnp.sum(weight, axis=1, keepdims=True)
            mixed = mixed + jnp.dot(weight.astype(BF16), kv[s, 1, cols, :], preferred_element_type=F32)
        og[:, 0:HD] = (mixed / mass).astype(BF16)
        kv_hop(s, 1)
        og[:, HD:512] = jax.nn.gelu(
            jnp.dot(hb[...], wi[...], preferred_element_type=F32), approximate=True
        ).astype(BF16)
        kv_hop(s, 2)
        if s > 0:
            def rs_sent(o, carry):
                block = tsend.at[my_slot, :]
                remote(block, block, rs_s.at[s - 1, o], rs_r.at[s - 1, o], partner).wait_send()
                return carry

            lax.fori_loop(1, CHIPS, rs_sent, 0)
        for n in range(4):
            cols = slice(384 * n, 384 * n + 384)
            upper = slice(HALF + 384 * n, HALF + 384 * n + 384)
            low = lax.dot_general(og[...], wo[cols, :], NT, preferred_element_type=F32)
            high = lax.dot_general(og[...], wo[upper, :], NT, preferred_element_type=F32)
            both = jnp.concatenate([low.reshape(CHIPS, 8, 384), high.reshape(CHIPS, 8, 384)], axis=1)
            tsend[:, cols] = both.reshape(CHIPS * 16, 384).astype(BF16)
        rland[s, my_slot, :] = tsend[my_slot, :]

        def rs_start(o, carry):
            yy, xx = chip_at(o)
            remote(
                tsend.at[slot(yy, xx), :], rland.at[s, my_slot, :], rs_s.at[s, o], rs_r.at[s, o],
                dev(yy, xx, c, z),
            ).start()
            return carry

        lax.fori_loop(1, CHIPS, rs_start, 0)
        kv_hop(s, 3)

        def rs_wait(o, carry):
            yy, xx = chip_from(o)
            remote(
                tsend.at[my_slot, :], rland.at[s, slot(yy, xx), :], rs_s.at[s, o], rs_r.at[s, o], partner
            ).wait_recv()
            return carry

        lax.fori_loop(1, 8, rs_wait, 0)
        kv_hop(s, 4)
        lax.fori_loop(8, CHIPS, rs_wait, 0)
        total = jnp.zeros((16, HALF), F32)
        for q in range(CHIPS):
            total = total + rland[s, 16 * q : 16 * q + 16, :].astype(F32)
        level = [sigma(jnp.full((16, HD), times[s + i].astype(F32))) for i in range(2)]
        gap = (level[1] - level[0])[:, 0:1]
        xp[...] = xp[...] + gap * total
        if s < STEPS - 1:
            ag_start(s + 1)
            kv_hop(s, 5)
            ag_wait(s + 1, 1, 6)
            kv_hop(s, 6)
            ag_wait(s + 1, 6, 11)
            kv_hop(s, 7)
            ag_wait(s + 1, 11, CHIPS)
            unpack(s + 1)
            kv_hop(s, 8)
            kv_wait(s)

    for r in range(CHIPS):
        k = r // 2
        first = 384 * (k % 4) + HD * (r % 2)
        fs[r] = xp[8 * (k // 4) : 8 * (k // 4) + 8, first : first + 256]

    def f_copy(r):
        rows = pl.ds(pl.multiple_of(me * 8, 8), 8)
        return remote(fs.at[r], fl.at[rows, :], f_s.at[r], f_r.at[me], (c * Z + z, r))

    def f_self():
        rows = pl.ds(pl.multiple_of(me * 8, 8), 8)
        return pltpu.make_async_copy(fs.at[head], fl.at[rows, :], f_r.at[me])

    def f_start(o, carry):
        r = lax.rem(head + o, CHIPS)
        f_copy(r).start()
        return carry

    lax.fori_loop(1, CHIPS, f_start, 0)

    @pl.when(natural)
    def _():
        f_self().start()

    @pl.when(jnp.logical_not(natural))
    def _():
        f_copy(head).start()

    def f_wait(q, carry):
        rows = pl.ds(pl.multiple_of(q * 8, 8), 8)
        remote(fs.at[0], fl.at[rows, :], f_s.at[0], f_r.at[q], partner).wait_recv()
        return carry

    lax.fori_loop(0, CHIPS, f_wait, 0)
    xt[...] = fl[...].T
    out[...] = xt[place, :]

    def all_sent(o, carry):
        remote(xs.at[0], xl.at[0], x_s.at[lax.rem(me + o, CHIPS)], x_r.at[0], partner).wait_send()
        f_copy(lax.rem(head + o, CHIPS)).wait_send()
        for s in range(STEPS):
            block = hland.at[s, my_slot, :]
            remote(block, block, ag_s.at[s, o], ag_r.at[s, o], partner).wait_send()
        block = tsend.at[my_slot, :]
        remote(block, block, rs_s.at[STEPS - 1, o], rs_r.at[STEPS - 1, o], partner).wait_send()
        return carry

    lax.fori_loop(1, CHIPS, all_sent, 0)

    @pl.when(jnp.logical_not(natural))
    def _():
        x_copy(me, partner).wait_send()
        f_copy(head).wait_send()
        for i, (src, here, there) in enumerate(shard_parts()):
            remote(src, there, swap_s.at[i], swap_r.at[i], twin).wait_send()

    def ring_sent(k, carry):
        for j in range(3):
            for d in range(2):
                ring_copy(j, d, k, z).wait_send()
        return carry

    lax.fori_loop(0, 7, ring_sent, 0)
    for j in range(3):
        for d in range(2):
            ring_copy(j, d, 7, z, d).wait_send()

    def pair_sent(zz, carry):
        for j in range(3):
            pair_copy(j, zz).wait_send()
        return carry

    lax.fori_loop(0, Z, pair_sent, 0)


def on_device(
    state, mod_weight, w_qkv, q_gain, k_gain, w_in, w_attn, w_out, cache_keys, cache_values, timesteps
):
    vmem = pl.BlockSpec(memory_space=pltpu.VMEM)
    hbm = pl.BlockSpec(memory_space=pl.ANY)
    smem = pl.BlockSpec(memory_space=pltpu.SMEM)
    dma = pltpu.SemaphoreType.DMA
    result = pl.pallas_call(
        kernel,
        out_shape=jax.ShapeDtypeStruct((192, TOK), F32),
        in_specs=[smem, vmem, vmem, hbm, hbm, hbm, hbm, hbm, hbm, hbm, hbm],
        out_specs=vmem,
        scratch_shapes=[
            pltpu.VMEM((D, 384), BF16),
            pltpu.VMEM((D, 384), BF16),
            pltpu.VMEM((D, 512), BF16),
            pltpu.VMEM((STEPS, 2, KEYS, HD), BF16),
            pltpu.VMEM((STEPS, CHIPS * 16, HALF), BF16),
            pltpu.VMEM((STEPS, CHIPS * 16, HALF), BF16),
            pltpu.VMEM((CHIPS * 16, HALF), BF16),
            pltpu.VMEM((TOK, D), BF16),
            pltpu.VMEM((TOK, 512), BF16),
            pltpu.VMEM((TOK, KEYS), F32),
            pltpu.VMEM((CHIPS, 16, 256), F32),
            pltpu.VMEM((CHIPS, 16, 256), F32),
            pltpu.VMEM((CHIPS, 8, 256), F32),
            pltpu.VMEM((TOK, 256), F32),
            pltpu.VMEM((256, TOK), F32),
            pltpu.VMEM((2, 256, 256), BF16),
            pltpu.VMEM((6, 16, HALF), F32),
            pltpu.VMEM((16, HALF), F32),
            pltpu.VMEM((2, 1, HD), F32),
            dma((4,)), dma((4,)), dma((4,)), dma((4,)),
            dma((3, 2, 8)), dma((3, 2, 8)), dma((3, Z)), dma((3, Z)),
            dma((2, 2, 8)), dma((2, 2, 8)), dma((2, Z)), dma((2, Z)),
            dma((CHIPS,)), dma((CHIPS,)),
            dma((STEPS, CHIPS)), dma((STEPS, CHIPS)), dma((STEPS, CHIPS)), dma((STEPS, CHIPS)),
            dma((CHIPS,)), dma((CHIPS,)), dma((4,)),
        ],
        compiler_params=pltpu.CompilerParams(
            collective_id=0, has_side_effects=True, vmem_limit_bytes=48 * 1024 * 1024
        ),
    )(
        timesteps,
        state.T,
        jnp.transpose(mod_weight, (1, 2, 0)),
        w_qkv.reshape(ROWS, 384),
        w_in,
        w_attn.T,
        w_out.T,
        q_gain,
        k_gain,
        cache_keys.reshape(KEYS, HD),
        cache_values.reshape(KEYS, HD),
    )
    return result.T


def solution(mesh):
    in_specs = (
        P("patch", "head"),
        P(None, None, "head"),
        P("patch", "head", None),
        P("head", None),
        P("head", None),
        P("patch", "head"),
        P("head", "patch"),
        P("head", "patch"),
        P(None, "head", None),
        P(None, "head", None),
        P(),
    )
    return jax.shard_map(
        on_device, mesh=mesh, in_specs=in_specs, out_specs=P("patch", "head"), check_vma=False
    )
```

time: 1620 us -> 175 us (0.11)
  waiting for transfers between devices: 1400 us -> 0 us
  Pallas kernels: 0 us -> 166 us
  blocking collectives: 127 us -> 0 us
  matrix products: 43.3 us -> 0 us
  other arithmetic: 27 us -> 0 us
  between operations: 16.3 us -> 0.02 us
    all_gather x10 -> x0, waiting for transfers between devices: 904 us -> none  [the longest x2 248 us: on_device(): lax.all_gather(delta_keys, 'patch', axis=0, tiled=True)]
    psum x3 -> x0, waiting for transfers between devices: 491 us -> none  [on_device(): summed = lax.psum(term.astype(jnp.bfloat16), 'head').astype(jnp.float32)]
    pallas_call x0 -> x1, Pallas kernels: none -> 166 us  [on_device(): pl.pallas_call(kernel, out_shape=jax.ShapeDtypeStruct((192, TOK), F32), i...]
    all_gather x4 -> x0, blocking collectives: 127 us -> none  [the longest x3 68 us: on_device(): lax.all_gather(mod_local, 'head', axis=1, tiled=True)]
    dot_general x15 -> x0, matrix products: 43.3 us -> none  [the longest x3 16.9 us: on_device(): jnp.dot(hidden, out_cols, preferred_element_type=jnp.float32)]
  transfers between devices with their start and end apart: 13 -> 0, of which waited for: 13 -> 0; matrix products, arithmetic and copies ran while one was open for 2% -> 0% of each run, Pallas kernels for 0% -> 0%
where the time goes in v1:
time: 175 us
  Pallas kernels  166 us (95%)
  local copies, waits for them, and re-layouts  8.98 us (5%)
    pallas_call x1, Pallas kernels, on_device(): pl.pallas_call(kernel, out_shape=jax.ShapeDtypeStruct((192, TOK), F32), i...  166 us
    unnamed x23, local copies, waits for them, and re-layouts  8.98 us

profile of v1, /device:TPU:1, one launch (start us, length us, event | category | flops | bytes accessed | tf_op | source)
XLA Modules:
  0.0 174.8 jit_solution(17140496609755990528)
XLA Ops:
  0.0 0.0 copy-start.8
  0.0 0.0 copy-start.9
  0.0 0.0 copy-start.10
  0.0 0.6 copy-done.8
  0.7 0.0 copy-done.9
  0.7 0.0 copy-done.10
  0.7 0.0 copy-start
  0.7 1.2 copy-done
  1.9 0.0 copy-start.1
  1.9 1.2 copy-done.1
  3.1 0.0 copy-start.2
  3.1 0.9 copy-done.2
  4.1 0.0 copy-start.3
  4.1 0.9 copy-done.3
  5.0 0.0 copy-start.4
  5.0 0.9 copy-done.4
  5.8 0.0 copy-start.5
  5.8 0.9 copy-done.5
  6.7 0.0 copy-start.6
  6.7 0.9 copy-done.6
  7.6 0.0 copy-start.7
  7.6 0.7 copy-done.7
  8.4 165.8 %shard_map.109 = f32[192,128]{1,0:T(8,128)S(1)} custom-call(s32[4]{0:T(128)S(1)} %copy-done.8, f32[192,128]{1,0:T(8,128)S(1)} %bitcast.12, bf16[2,192,256]{2,1,0:T(8,128)(2,1)S(1)} %bitcast.11, bf16[96,384]{1,0:T(8,128)(2,1)S(1)} %bitcast.13, bf16[96,384]{1,0:T(8,128)(2,1)S(1)} %copy-done.5, bf16[96,128]{1,0:T(8,128)(2,1)S(1)} %bitcast.15, ...), custom_call_target="tpu_custom_call" | custom-call | tf_op jit(solution)/shard_map/pallas_call | solution.py:533
  174.2 0.6 copy.13
Async XLA Ops:
  0.0 0.7 copy-start.8
  0.0 0.7 copy-start.9
  0.0 0.7 copy-start.10
  0.7 1.2 copy-start
  1.9 1.2 copy-start.1
  3.1 0.9 copy-start.2
  4.1 0.9 copy-start.3
  5.0 0.9 copy-start.4
  5.8 0.9 copy-start.5
  6.7 0.9 copy-start.6
  7.6 0.7 copy-start.7

commit v2 on v1

--- a/solution.py
+++ b/solution.py
@@ -17,6 +17,7 @@
 TOK = 128
 D = 3072
 HALF = D // 2
+PART = HALF // 2
 HD = 128
 ROWS = 96
 KEYS = 4096
@@ -32,9 +33,10 @@
 def kernel(
     times, state, mod_w, w_qkv, w_in, w_attn, w_out, q_gain, k_gain, cache_k, cache_v,
     out,
-    wq, wi, wo, kv, hland, rland, tsend, hb, og, scores, xs, xl, fs, fl, xt, mw, modp, xp, gains,
+    wq, wi, wo, kv, hland, r1, r2, tsend, p2, hb, og, scores, xs, xl, fs, fl, xt, mw, modp, xp, gains,
     cache_s, cache_r, swap_s, swap_r, ring_s, ring_r, pair_s, pair_r,
-    kring_s, kring_r, kpair_s, kpair_r, x_s, x_r, ag_s, ag_r, rs_s, rs_r, f_s, f_r, local,
+    kring_s, kring_r, kpair_s, kpair_r, x_s, x_r, ag1_s, ag1_r, ag2_s, ag2_r,
+    rs1_s, rs1_r, rs2_s, rs2_r, f_s, f_r, local,
 ):
     patch = lax.axis_index("patch")
     head = lax.axis_index("head")
@@ -51,9 +53,6 @@
     def chip_at(o):
         return lax.rem(y + lax.div(o, 4), 4), lax.rem(x + lax.rem(o, 4), 4)
 
-    def chip_from(o):
-        return lax.rem(y + 4 - lax.div(o, 4), 4), lax.rem(x + 4 - lax.rem(o, 4), 4)
-
     def remote(src, dst, send, recv, device):
         return pltpu.make_async_remote_copy(
             src_ref=src, dst_ref=dst, send_sem=send, recv_sem=recv, device_id=device, device_id_type=MESH
@@ -61,6 +60,7 @@
 
     partner = dev(y, x, 1 - c, z)
     z_next = (dev(y, x, c, lax.rem(z + 1, Z)), dev(y, x, c, lax.rem(z + Z - 1, Z)))
+    z_far = (dev(y, x, c, lax.rem(z + 2, Z)), dev(y, x, c, lax.rem(z + Z - 2, Z)))
     twin = dev(yh * 2 + c, x, yl, z)
 
     barrier = pltpu.get_barrier_semaphore()
@@ -74,8 +74,8 @@
         greet(dev(yy, xx, 1 - c, z))
         return carry
 
-    greet(z_next[0])
-    greet(z_next[1])
+    for device in z_next + z_far:
+        greet(device)
     greet(partner)
     lax.fori_loop(1, CHIPS, greet_chip, 0)
 
@@ -105,68 +105,13 @@
             (k_gain, gains.at[1]),
         )
 
-    pl.semaphore_wait(barrier, 33)
-
-    for i, (src, here, there) in enumerate(shard_parts()):
-        @pl.when(natural)
-        def _():
+
+    @pl.when(natural)
+    def _():
+        for i, (src, here, there) in enumerate(shard_parts()):
             pltpu.make_async_copy(src, here, swap_r.at[i]).start()
-
-        @pl.when(jnp.logical_not(natural))
-        def _():
-            remote(src, there, swap_s.at[i], swap_r.at[i], twin).start()
-
-    @pl.when(natural)
-    def _():
         for i, (src, dst) in enumerate(caches()):
             pltpu.make_async_copy(src, dst, local.at[i]).start()
-            remote(src, dst, cache_s.at[i], cache_r.at[i], partner).start()
-
-    def wait_own(i):
-        src, here, there = shard_parts()[i]
-        pltpu.make_async_copy(src, here, swap_r.at[i]).wait()
-
-    def pair_copy(j, zz):
-        part = slab(j, zz)
-        return remote(part, part, pair_s.at[j, zz], pair_r.at[j, zz], partner)
-
-    def pair_wait(j, zz):
-        start = pl.multiple_of(((1 - c) * Z + zz) * ROWS, 16)
-        part = weights[j].at[pl.ds(start, ROWS), :]
-        remote(part, part, pair_s.at[j, zz], pair_r.at[j, zz], partner).wait_recv()
-
-    def ring_copy(j, d, k, zz, part=None):
-        block = slab(j, zz, part)
-        return remote(block, block, ring_s.at[j, d, k], ring_r.at[j, d, k], z_next[d])
-
-    def source(d, k):
-        return lax.rem(z + Z - k, Z) if d == 0 else lax.rem(z + k, Z)
-
-    def ring_start():
-        for j in range(3):
-            wait_own(j)
-            if j == 2:
-                wait_own(3)
-            for d in range(2):
-                ring_copy(j, d, 0, z).start()
-            pair_copy(j, z).start()
-
-    def ring_hop(k, last=False):
-        for j in range(3):
-            for d in range(2):
-                zz = source(d, k)
-                ring_copy(j, d, k - 1, zz).wait_recv()
-                ring_copy(j, d, k, zz, d if last else None).start()
-                pair_copy(j, zz).start()
-
-    def ring_end():
-        zz = source(0, 8)
-        for j in range(3):
-            for d in range(2):
-                ring_copy(j, d, 7, zz, d).wait_recv()
-            pair_copy(j, zz).start()
-
-    ring_start()
 
     row = lax.broadcasted_iota(jnp.int32, (8, HD), 0)
     lane = lax.broadcasted_iota(jnp.int32, (8, HD), 1)
@@ -191,6 +136,70 @@
         xs[q, 0:8] = rows_here[8 * q : 8 * q + 8]
         xs[q, 8:16] = mod_rows
 
+    pl.semaphore_wait(barrier, 35)
+
+    @pl.when(jnp.logical_not(natural))
+    def _():
+        for i, (src, here, there) in enumerate(shard_parts()):
+            remote(src, there, swap_s.at[i], swap_r.at[i], twin).start()
+
+    @pl.when(natural)
+    def _():
+        for i, (src, dst) in enumerate(caches()):
+            remote(src, dst, cache_s.at[i], cache_r.at[i], partner).start()
+
+    def wait_own(i):
+        src, here, there = shard_parts()[i]
+        pltpu.make_async_copy(src, here, swap_r.at[i]).wait()
+
+    def pair_copy(j, zz):
+        part = slab(j, zz)
+        return remote(part, part, pair_s.at[j, zz], pair_r.at[j, zz], partner)
+
+    def pair_wait(j, zz):
+        start = pl.multiple_of(((1 - c) * Z + zz) * ROWS, 16)
+        part = weights[j].at[pl.ds(start, ROWS), :]
+        remote(part, part, pair_s.at[j, zz], pair_r.at[j, zz], partner).wait_recv()
+
+    def ring_copy(j, d, k, zz, part=None):
+        block = slab(j, zz, part)
+        return remote(block, block, ring_s.at[j, d, k], ring_r.at[j, d, k], z_next[d])
+
+    def source(d, k):
+        return lax.rem(z + Z - k, Z) if d == 0 else lax.rem(z + k, Z)
+
+    def ring_start():
+        for j in range(3):
+            wait_own(j)
+            if j == 2:
+                wait_own(3)
+            for d in range(2):
+                ring_copy(j, d, 0, z).start()
+            pair_copy(j, z).start()
+
+    def ring_hop(k, last=False):
+        for j in range(3):
+            for d in range(2):
+                zz = source(d, k)
+                ring_copy(j, d, k - 1, zz).wait_recv()
+                ring_copy(j, d, k, zz, d if last else None).start()
+                pair_copy(j, zz).start()
+
+    def ring_end(j):
+        zz = source(0, 8)
+        for d in range(2):
+            ring_copy(j, d, 7, zz, d).wait_recv()
+        pair_copy(j, zz).start()
+
+    def pair_all(j):
+        def body(zz, carry):
+            pair_wait(j, zz)
+            return carry
+
+        lax.fori_loop(0, Z, body, 0)
+
+    ring_start()
+
     def x_copy(q, device):
         return remote(xs.at[q], xl.at[head], x_s.at[q], x_r.at[head], device)
 
@@ -235,55 +244,120 @@
         total = (sums[0:8] + sums[8:16]) * (1.0 / D)
         return jnp.concatenate([total, total], axis=0)
 
-    my_slot = pl.ds(pl.multiple_of(me * 16, 16), 16)
+    def turn(i, d):
+        return lax.rem(i + d, 4)
 
     def slot(yy, xx):
         return pl.ds(pl.multiple_of((yy * 4 + xx) * 16, 16), 16)
+
+    def line(half, d):
+        return dev(y, turn(x, d), c, z) if half == 0 else dev(turn(y, d), x, c, z)
+
+    def origin(half, d1, d2=0):
+        dy, dx = (d2, d1) if half == 0 else (d1, d2)
+        return slot(turn(y, 4 - dy), turn(x, 4 - dx))
+
+    def ag1(s, half, d, rows):
+        block = hland.at[s, half, rows, :]
+        return remote(block, block, ag1_s.at[s, half, d], ag1_r.at[s, half, d], line(half, d))
+
+    def ag2(s, half, d1, d2, rows):
+        block = hland.at[s, half, rows, :]
+        i = d1 * 4 + d2
+        return remote(block, block, ag2_s.at[s, half, i], ag2_r.at[s, half, i], line(1 - half, d2))
 
     def ag_start(s):
         rows = xp[...]
         delta = rows - fold(jnp.sum(rows, axis=1, keepdims=True))
         var = fold(jnp.sum(delta * delta, axis=1, keepdims=True))
-        h = delta * lax.rsqrt(var + 1e-06) * (1.0 + modp[s]) + modp[3 + s]
-        hland[s, my_slot, :] = h.astype(BF16)
-
-        def body(o, carry):
-            yy, xx = chip_at(o)
-            block = hland.at[s, my_slot, :]
-            remote(block, block, ag_s.at[s, o], ag_r.at[s, o], dev(yy, xx, c, z)).start()
-            return carry
-
-        lax.fori_loop(1, CHIPS, body, 0)
-
-    def ag_wait(s, lo=1, hi=CHIPS):
-        def body(o, carry):
-            yy, xx = chip_from(o)
-            block = hland.at[s, slot(yy, xx), :]
-            remote(block, block, ag_s.at[s, o], ag_r.at[s, o], partner).wait_recv()
-            return carry
-
-        lax.fori_loop(lo, hi, body, 0)
-
-    def unpack(s):
+        h = (delta * lax.rsqrt(var + 1e-06) * (1.0 + modp[s]) + modp[3 + s]).astype(BF16)
+        mine = slot(y, x)
+        for half in range(2):
+            hland[s, half, mine, :] = h[:, half * PART : half * PART + PART]
+        for d in (1, 3, 2):
+            for half in range(2):
+                ag1(s, half, d, mine).start()
+        for d in (1, 3, 2):
+            for half in range(2):
+                ag2(s, half, 0, d, mine).start()
+
+    def ag_forward(s):
+        for d in (1, 3, 2):
+            for half in range(2):
+                rows = origin(half, d)
+                ag1(s, half, d, rows).wait_recv()
+                for e in (1, 3, 2):
+                    ag2(s, half, d, e, rows).start()
+
+    def ag_end(s, half):
+        for d in (0, 1, 3, 2):
+            for e in (1, 3, 2):
+                ag2(s, half, d, e, origin(half, d, e)).wait_recv()
+
+    def ag_sent(s):
+        mine = slot(y, x)
+        for half in range(2):
+            for e in (1, 2, 3):
+                ag1(s, half, e, mine).wait_send()
+                for d in range(4):
+                    ag2(s, half, d, e, mine).wait_send()
+
+    def rs1(s, half, d):
+        to = turn(y if half == 0 else x, d)
+        block = tsend.at[half, pl.ds(pl.multiple_of(to * 64, 64), 64), :]
+        return remote(
+            block, r1.at[s, half, d - 1], rs1_s.at[s, half, d], rs1_r.at[s, half, d], line(1 - half, d)
+        )
+
+    def rs2(s, half, d):
+        to = turn(x if half == 0 else y, d)
+        block = p2.at[half, pl.ds(pl.multiple_of(to * 16, 16), 16), :]
+        return remote(
+            block, r2.at[s, half, d - 1], rs2_s.at[s, half, d], rs2_r.at[s, half, d], line(half, d)
+        )
+
+    def rs_middle(s):
+        for half in range(2):
+            here = pl.ds(pl.multiple_of((y if half == 0 else x) * 64, 64), 64)
+            for d in (1, 3, 2):
+                rs1(s, half, d).wait_recv()
+            part = tsend[half, here, :].astype(F32)
+            for d in range(3):
+                part = part + r1[s, half, d].astype(F32)
+            p2[half] = part.astype(BF16)
+            for d in (1, 3, 2):
+                rs2(s, half, d).start()
+
+    def rs_end(s):
+        parts = []
+        for half in range(2):
+            here = pl.ds(pl.multiple_of((x if half == 0 else y) * 16, 16), 16)
+            part = p2[half, here, :].astype(F32)
+            for d in (1, 3, 2):
+                rs2(s, half, d).wait_recv()
+                part = part + r2[s, half, d - 1].astype(F32)
+            parts.append(part)
+        return jnp.concatenate(parts, axis=1)
+
+    def unpack(s, half):
         for m in range(8):
-            block = hland[s, 32 * m : 32 * m + 32, :].astype(F32)
+            block = hland[s, half, 32 * m : 32 * m + 32, :].astype(F32)
             rows = slice(16 * m, 16 * m + 16)
-            hb[rows, 0:HALF] = jnp.concatenate([block[0:8], block[16:24]], axis=0).astype(BF16)
-            hb[rows, HALF:D] = jnp.concatenate([block[8:16], block[24:32]], axis=0).astype(BF16)
+            low, high = half * PART, HALF + half * PART
+            hb[rows, low : low + PART] = jnp.concatenate([block[0:8], block[16:24]], axis=0).astype(BF16)
+            hb[rows, high : high + PART] = jnp.concatenate([block[8:16], block[24:32]], axis=0).astype(BF16)
 
     ag_start(0)
-    loop_hops(3, 7)
-    ag_wait(0)
-    unpack(0)
+    loop_hops(3, 5)
+    ag_forward(0)
+    loop_hops(5, 7)
+    for half in range(2):
+        ag_end(0, half)
+        unpack(0, half)
     ring_hop(7, last=True)
-    ring_end()
-
-    def pair_loop(zz, carry):
-        for j in range(3):
-            pair_wait(j, zz)
-        return carry
-
-    lax.fori_loop(0, Z, pair_loop, 0)
+    ring_end(0)
+    ring_end(1)
+    pair_all(0)
 
     @pl.when(natural)
     def _():
@@ -302,32 +376,37 @@
             start, size = start + part * (TOK // 2), TOK // 2
         return kv.at[s + 1, :, pl.ds(pl.multiple_of(start, 16), size), :]
 
-    def kring_copy(s, d, k, zz, part=None):
+    def kring_copy(s, d, k, far, zz, part=None):
         block = kv_block(s, c, zz, part)
-        return remote(block, block, kring_s.at[s, d, k], kring_r.at[s, d, k], z_next[d])
+        device = z_far[d] if far else z_next[d]
+        return remote(block, block, kring_s.at[s, d, k, far], kring_r.at[s, d, k, far], device)
 
     def kpair_copy(s, zz):
         block = kv_block(s, c, zz)
         return remote(block, block, kpair_s.at[s, zz], kpair_r.at[s, zz], partner)
 
+    def kv_send(s, k):
+        for d in range(2):
+            kring_copy(s, d, k, 1, source(d, 2 * k), d if k == 3 else None).start()
+        for d in range(2):
+            kring_copy(s, d, k, 0, source(d, 2 * k)).start()
+
     def kv_start(s):
-        for d in range(2):
-            kring_copy(s, d, 0, z).start()
+        kv_send(s, 0)
         kpair_copy(s, z).start()
 
-    def kv_hop(s, k):
-        if s >= STEPS - 1:
-            return
-        if k < 8:
+    def kv_stage(s, k):
+        for d in range(2):
+            kring_copy(s, d, k - 1, 1, source(d, 2 * k), d if k == 4 else None).wait_recv()
+        if k < 4:
+            kv_send(s, k)
             for d in range(2):
-                zz = source(d, k)
-                kring_copy(s, d, k - 1, zz).wait_recv()
-                kring_copy(s, d, k, zz, d if k == 7 else None).start()
-                kpair_copy(s, zz).start()
+                kpair_copy(s, source(d, 2 * k)).start()
         else:
-            zz = source(0, 8)
-            for d in range(2):
-                kring_copy(s, d, 7, zz, d).wait_recv()
+            kpair_copy(s, source(0, 8)).start()
+        for d in range(2):
+            zz = source(d, 2 * k - 1)
+            kring_copy(s, d, k - 1, 0, zz).wait_recv()
             kpair_copy(s, zz).start()
 
     def kv_wait(s):
@@ -338,21 +417,23 @@
 
         lax.fori_loop(0, Z, body, 0)
 
-    def kv_sent(s):
-        def body(k, carry):
-            for d in range(2):
-                kring_copy(s, d, k, z).wait_send()
+    def kv_sent_own(s):
+        for d in range(2):
+            for far in range(2):
+                kring_copy(s, d, 0, far, z).wait_send()
+        kpair_copy(s, z).wait_send()
+
+    def kv_sent_rest(s):
+        for d in range(2):
+            for k in range(1, 4):
+                kring_copy(s, d, k, 0, z).wait_send()
+                kring_copy(s, d, k, 1, z, d if k == 3 else None).wait_send()
+
+        def pairs(o, carry):
+            kpair_copy(s, lax.rem(z + o, Z)).wait_send()
             return carry
 
-        lax.fori_loop(0, 7, body, 0)
-        for d in range(2):
-            kring_copy(s, d, 7, z, d).wait_send()
-
-        def pairs(zz, carry):
-            kpair_copy(s, zz).wait_send()
-            return carry
-
-        lax.fori_loop(0, Z, pairs, 0)
+        lax.fori_loop(1, Z, pairs, 0)
 
     def rms(values, gain):
         return values * lax.rsqrt(jnp.mean(values * values, axis=1, keepdims=True) + 1e-06) * gain
@@ -364,7 +445,7 @@
         query = rms(qkv[:, 0:HD], gains[0]).astype(BF16)
         fresh = (rms(qkv[:, HD : 2 * HD], gains[1]).astype(BF16), qkv[:, 2 * HD :].astype(BF16))
         if s > 0:
-            kv_sent(s - 1)
+            kv_sent_own(s - 1)
         for i in range(2):
             old = kv[s, i, own_rows, :].astype(F32)
             if s < STEPS - 1:
@@ -373,6 +454,16 @@
             kv[s, i, own_rows, :] = fresh[i]
         if s < STEPS - 1:
             kv_start(s)
+        if s == 0:
+            pair_all(1)
+        og[:, HD:512] = jax.nn.gelu(
+            jnp.dot(hb[...], wi[...], preferred_element_type=F32), approximate=True
+        ).astype(BF16)
+        if s == 0:
+            ring_end(2)
+        else:
+            kv_stage(s - 1, 4)
+            kv_wait(s - 1)
         top = jnp.full((TOK, 1), -jnp.inf, F32)
         for j in range(KEYS // CHUNK):
             cols = slice(CHUNK * j, CHUNK * j + CHUNK)
@@ -388,65 +479,43 @@
             mass = mass + jnp.sum(weight, axis=1, keepdims=True)
             mixed = mixed + jnp.dot(weight.astype(BF16), kv[s, 1, cols, :], preferred_element_type=F32)
         og[:, 0:HD] = (mixed / mass).astype(BF16)
-        kv_hop(s, 1)
-        og[:, HD:512] = jax.nn.gelu(
-            jnp.dot(hb[...], wi[...], preferred_element_type=F32), approximate=True
-        ).astype(BF16)
-        kv_hop(s, 2)
-        if s > 0:
-            def rs_sent(o, carry):
-                block = tsend.at[my_slot, :]
-                remote(block, block, rs_s.at[s - 1, o], rs_r.at[s - 1, o], partner).wait_send()
-                return carry
-
-            lax.fori_loop(1, CHIPS, rs_sent, 0)
+        if s == 0:
+            pair_all(2)
+        else:
+            for half in range(2):
+                for d in (1, 2, 3):
+                    rs1(s - 1, half, d).wait_send()
+                    rs2(s - 1, half, d).wait_send()
         for n in range(4):
+            half, first = n // 2, 384 * (n % 2)
             cols = slice(384 * n, 384 * n + 384)
             upper = slice(HALF + 384 * n, HALF + 384 * n + 384)
             low = lax.dot_general(og[...], wo[cols, :], NT, preferred_element_type=F32)
             high = lax.dot_general(og[...], wo[upper, :], NT, preferred_element_type=F32)
-            both = jnp.concatenate([low.reshape(CHIPS, 8, 384), high.reshape(CHIPS, 8, 384)], axis=1)
-            tsend[:, cols] = both.reshape(CHIPS * 16, 384).astype(BF16)
-        rland[s, my_slot, :] = tsend[my_slot, :]
-
-        def rs_start(o, carry):
-            yy, xx = chip_at(o)
-            remote(
-                tsend.at[slot(yy, xx), :], rland.at[s, my_slot, :], rs_s.at[s, o], rs_r.at[s, o],
-                dev(yy, xx, c, z),
-            ).start()
-            return carry
-
-        lax.fori_loop(1, CHIPS, rs_start, 0)
-        kv_hop(s, 3)
-
-        def rs_wait(o, carry):
-            yy, xx = chip_from(o)
-            remote(
-                tsend.at[my_slot, :], rland.at[s, slot(yy, xx), :], rs_s.at[s, o], rs_r.at[s, o], partner
-            ).wait_recv()
-            return carry
-
-        lax.fori_loop(1, 8, rs_wait, 0)
-        kv_hop(s, 4)
-        lax.fori_loop(8, CHIPS, rs_wait, 0)
-        total = jnp.zeros((16, HALF), F32)
-        for q in range(CHIPS):
-            total = total + rland[s, 16 * q : 16 * q + 16, :].astype(F32)
+            for q in range(CHIPS):
+                rows = slice(8 * q, 8 * q + 8)
+                spot = 16 * (q if half == 0 else 4 * (q % 4) + q // 4)
+                both = jnp.concatenate([low[rows], high[rows]], axis=0).astype(BF16)
+                tsend[half, spot : spot + 16, first : first + 384] = both
+            if n % 2 == 1:
+                for d in (1, 3, 2):
+                    rs1(s, half, d).start()
+        if s < STEPS - 1:
+            kv_stage(s, 1)
+        rs_middle(s)
+        if s < STEPS - 1:
+            kv_stage(s, 2)
+        total = rs_end(s)
         level = [sigma(jnp.full((16, HD), times[s + i].astype(F32))) for i in range(2)]
         gap = (level[1] - level[0])[:, 0:1]
         xp[...] = xp[...] + gap * total
         if s < STEPS - 1:
             ag_start(s + 1)
-            kv_hop(s, 5)
-            ag_wait(s + 1, 1, 6)
-            kv_hop(s, 6)
-            ag_wait(s + 1, 6, 11)
-            kv_hop(s, 7)
-            ag_wait(s + 1, 11, CHIPS)
-            unpack(s + 1)
-            kv_hop(s, 8)
-            kv_wait(s)
+            kv_stage(s, 3)
+            ag_forward(s + 1)
+            for half in range(2):
+                ag_end(s + 1, half)
+                unpack(s + 1, half)
 
     for r in range(CHIPS):
         k = r // 2
@@ -488,14 +557,17 @@
     def all_sent(o, carry):
         remote(xs.at[0], xl.at[0], x_s.at[lax.rem(me + o, CHIPS)], x_r.at[0], partner).wait_send()
         f_copy(lax.rem(head + o, CHIPS)).wait_send()
-        for s in range(STEPS):
-            block = hland.at[s, my_slot, :]
-            remote(block, block, ag_s.at[s, o], ag_r.at[s, o], partner).wait_send()
-        block = tsend.at[my_slot, :]
-        remote(block, block, rs_s.at[STEPS - 1, o], rs_r.at[STEPS - 1, o], partner).wait_send()
         return carry
 
     lax.fori_loop(1, CHIPS, all_sent, 0)
+    for s in range(STEPS):
+        ag_sent(s)
+    for s in range(STEPS - 1):
+        kv_sent_rest(s)
+    for half in range(2):
+        for d in (1, 2, 3):
+            rs1(STEPS - 1, half, d).wait_send()
+            rs2(STEPS - 1, half, d).wait_send()
 
     @pl.when(jnp.logical_not(natural))
     def _():
@@ -540,9 +612,11 @@
             pltpu.VMEM((D, 384), BF16),
             pltpu.VMEM((D, 512), BF16),
             pltpu.VMEM((STEPS, 2, KEYS, HD), BF16),
-            pltpu.VMEM((STEPS, CHIPS * 16, HALF), BF16),
-            pltpu.VMEM((STEPS, CHIPS * 16, HALF), BF16),
-            pltpu.VMEM((CHIPS * 16, HALF), BF16),
+            pltpu.VMEM((STEPS, 2, CHIPS * 16, PART), BF16),
+            pltpu.VMEM((STEPS, 2, 3, 64, PART), BF16),
+            pltpu.VMEM((STEPS, 2, 3, 16, PART), BF16),
+            pltpu.VMEM((2, CHIPS * 16, PART), BF16),
+            pltpu.VMEM((2, 64, PART), BF16),
             pltpu.VMEM((TOK, D), BF16),
             pltpu.VMEM((TOK, 512), BF16),
             pltpu.VMEM((TOK, KEYS), F32),
@@ -557,13 +631,14 @@
             pltpu.VMEM((2, 1, HD), F32),
             dma((4,)), dma((4,)), dma((4,)), dma((4,)),
             dma((3, 2, 8)), dma((3, 2, 8)), dma((3, Z)), dma((3, Z)),
-            dma((2, 2, 8)), dma((2, 2, 8)), dma((2, Z)), dma((2, Z)),
+            dma((2, 2, 4, 2)), dma((2, 2, 4, 2)), dma((2, Z)), dma((2, Z)),
             dma((CHIPS,)), dma((CHIPS,)),
-            dma((STEPS, CHIPS)), dma((STEPS, CHIPS)), dma((STEPS, CHIPS)), dma((STEPS, CHIPS)),
+            dma((STEPS, 2, 4)), dma((STEPS, 2, 4)), dma((STEPS, 2, 16)), dma((STEPS, 2, 16)),
+            dma((STEPS, 2, 4)), dma((STEPS, 2, 4)), dma((STEPS, 2, 4)), dma((STEPS, 2, 4)),
             dma((CHIPS,)), dma((CHIPS,)), dma((4,)),
         ],
         compiler_params=pltpu.CompilerParams(
-            collective_id=0, has_side_effects=True, vmem_limit_bytes=48 * 1024 * 1024
+            collective_id=0, has_side_effects=True, vmem_limit_bytes=60 * 1024 * 1024
         ),
     )(
         timesteps,

time: 175 us -> 138 us (0.79)
  Pallas kernels: 166 us -> 137 us
  local copies, waits for them, and re-layouts: 8.98 us -> 1.54 us
    pallas_call x1, Pallas kernels: 166 us -> 137 us  [on_device(): pl.pallas_call(kernel, out_shape=jax.ShapeDtypeStruct((192, TOK), F32), i...]
    unnamed x23 -> x1, local copies, waits for them, and re-layouts: 8.98 us -> 1.54 us
where the time goes in v2:
time: 138 us
  Pallas kernels  137 us (99%)
  local copies, waits for them, and re-layouts  1.54 us (1%)
    pallas_call x1, Pallas kernels, on_device(): pl.pallas_call(kernel, out_shape=jax.ShapeDtypeStruct((192, TOK), F32), i...  137 us

profile of v2, /device:TPU:1, one launch (start us, length us, event | category | flops | bytes accessed | tf_op | source)
XLA Modules:
  0.0 138.3 jit_solution(14841934956958243372)
XLA Ops:
  0.0 136.7 %shard_map.109 = f32[192,128]{1,0:T(8,128)} custom-call(s32[4]{0:T(128)} %times.1, f32[192,128]{1,0:T(8,128)} %bitcast.12, bf16[2,192,256]{2,1,0:T(8,128)(2,1)} %bitcast.11, bf16[96,384]{1,0:T(8,128)(2,1)} %bitcast.13, bf16[96,384]{1,0:T(8,128)(2,1)} %w_in.1, bf16[96,128]{1,0:T(8,128)(2,1)} %bitcast.15, bf16[96,384]{1,0:T(8,128)(2,1)} %bitcast.14, ...), custom_call_target="tpu_custom_call" | custom-call | tf_op jit(solution)/shard_map/pallas_call | solution.py:605
  136.7 1.5 %copy.13 = f32[128,192]{0,1:T(8,128)} copy(f32[128,192]{0,1:T(8,128)} %bitcast.10) | data formatting | bytes 196608

commit v3 on v2

v3 whole, which is shorter than its diff:
```python
import math

import jax
import jax.numpy as jnp
from jax import lax
from jax.experimental import pallas as pl
from jax.experimental.pallas import tpu as pltpu
from jax.sharding import PartitionSpec as P

MESH = pl.DeviceIdType.MESH
F32 = jnp.float32
BF16 = jnp.bfloat16
SCHED = 1000
STEPS = 3
Z = 16
CHIPS = 16
TOK = 128
D = 3072
HALF = D // 2
PART = HALF // 2
HD = 128
ROWS = 96
KEYS = 4096
CHUNK = 512
NT = (((1,), (1,)), ((), ()))


def sigma(unit_index):
    unit = 1.0 - unit_index / SCHED
    return 3.0 * unit / (1.0 + 2.0 * unit)


def kernel(
    times, state, mod_w, w_qkv, w_in, w_attn, w_out, q_gain, k_gain, cache_k, cache_v,
    out,
    wq, wi, wo, kv, hland, r1, r2, tsend, p2, hb, og, scores, xs, xl, fs, fl, tt, ft, xt, mw, modp, xp, gains,
    cache_s, cache_r, swap_s, swap_r, first_s, ring_s, ring_r, pair_s, pair_r,
    kring_s, kring_r, kpair_r, x_s, x_r, ag_s, ag1_r, ag2_r,
    rs1_s, rs1_r, rs2_s, rs2_r, f_s, f_r, t_s, t_r, local,
):
    patch = lax.axis_index("patch")
    head = lax.axis_index("head")
    yl, z = lax.div(patch, Z), lax.rem(patch, Z)
    yh, x, c = lax.div(head, 8), lax.rem(lax.div(head, 2), 4), lax.rem(head, 2)
    y = yh * 2 + yl
    me = y * 4 + x
    own = c * Z + z
    natural = c == yl

    def dev(yy, xx, cc, zz):
        return (lax.rem(yy, 2) * Z + zz, lax.div(yy, 2) * 8 + xx * 2 + cc)

    def chip_at(o):
        return lax.rem(y + lax.div(o, 4), 4), lax.rem(x + lax.rem(o, 4), 4)

    def remote(src, dst, send, recv, device):
        return pltpu.make_async_remote_copy(
            src_ref=src, dst_ref=dst, send_sem=send, recv_sem=recv, device_id=device, device_id_type=MESH
        )

    partner = dev(y, x, 1 - c, z)

    def wait_bytes(block, sem):
        pltpu.make_async_copy(block, block, sem).wait()

    z_next = (dev(y, x, c, lax.rem(z + 1, Z)), dev(y, x, c, lax.rem(z + Z - 1, Z)))
    z_far = (dev(y, x, c, lax.rem(z + 2, Z)), dev(y, x, c, lax.rem(z + Z - 2, Z)))
    twin = dev(yh * 2 + c, x, yl, z)
    twin_next = (dev(yh * 2 + c, x, yl, lax.rem(z + 1, Z)), dev(yh * 2 + c, x, yl, lax.rem(z + Z - 1, Z)))

    barrier = pltpu.get_barrier_semaphore()

    def greet(device):
        pl.semaphore_signal(barrier, inc=1, device_id=device, device_id_type=MESH)

    for device in z_next + z_far + twin_next:
        greet(device)
    rows_y = [lax.rem(y + d, 4) for d in range(4)]
    rows_x = [lax.rem(x + d, 4) for d in range(4)]
    greet(partner)
    for o in range(1, CHIPS):
        for core in range(2):
            greet(dev(rows_y[o // 4], rows_x[o % 4], core, z))

    weights = (wq, wi, wo)

    def slab(j, zz, half=None):
        start, size = (c * Z + zz) * ROWS, ROWS
        if half is not None:
            start, size = start + half * (ROWS // 2), ROWS // 2
        return weights[j].at[pl.ds(pl.multiple_of(start, 16), size), :]

    def shard(i, block):
        rows = pl.ds(pl.multiple_of(block * ROWS, 16), ROWS)
        return (
            (w_qkv, wq.at[rows, :]),
            (w_in, wi.at[rows, :]),
            (w_attn, wo.at[rows, 0:HD]),
            (w_out, wo.at[rows, HD:512]),
        )[i]

    def caches():
        return (
            (cache_k, kv.at[0, 0]),
            (cache_v, kv.at[0, 1]),
            (q_gain, gains.at[0]),
            (k_gain, gains.at[1]),
        )

    place = pl.ds(pl.multiple_of(c * 64, 64), 192)
    mw[...] = jnp.zeros_like(mw)
    xt[...] = jnp.zeros_like(xt)
    loads = [
        pltpu.make_async_copy(state, xt.at[place, :], local.at[0]),
        pltpu.make_async_copy(mod_w, mw.at[:, place, :], local.at[1]),
    ]
    for load in loads:
        load.start()

    pl.semaphore_wait(barrier, 37)

    for d in range(2):
        src, dst = shard(0, patch)
        remote(src, dst, first_s, ring_r.at[0, d, 0], twin_next[d]).start()
    part_of = (0, 1, 2, 2)

    @pl.when(natural)
    def _():
        for i in (1, 2, 3, 0):
            src, dst = shard(i, patch)
            pltpu.make_async_copy(src, dst, swap_r.at[part_of[i]]).start()
        for i, (src, dst) in enumerate(caches()):
            pltpu.make_async_copy(src, dst, cache_r.at[i // 2]).start()
            remote(src, dst, cache_s.at[i // 2], cache_r.at[i // 2], partner).start()

    @pl.when(jnp.logical_not(natural))
    def _():
        for i in (1, 2, 3, 0):
            src, dst = shard(i, patch)
            remote(src, dst, swap_s, swap_r.at[part_of[i]], twin).start()

    def pair_copy(j, zz):
        part = slab(j, zz)
        return remote(part, part, pair_s.at[j], pair_r.at[j], partner)

    def ring_copy(j, d, k, zz, half=None):
        block = slab(j, zz, half)
        return remote(block, block, ring_s.at[j], ring_r.at[j, d, lax.rem(k, 2)], z_next[d])

    def source(d, k):
        return lax.rem(z + Z - k, Z) if d == 0 else lax.rem(z + k, Z)

    def ring_start(j):
        wait_bytes(slab(j, z), swap_r.at[j])
        if j > 0:
            for d in range(2):
                ring_copy(j, d, 0, z).start()
        pair_copy(j, z).start()

    def ring_hop(k, last=False):
        for j in range(3):
            for d in range(2):
                ring_copy(j, d, k - 1, source(d, k)).wait_recv()
            for d in range(2):
                ring_copy(j, d, k, source(d, k), d if last else None).start()
            for d in range(2):
                pair_copy(j, source(d, k)).start()

    def ring_end(j):
        zz = source(0, 8)
        for d in range(2):
            ring_copy(j, d, 7, zz, d).wait_recv()
        pair_copy(j, zz).start()

    def pair_all(j):
        rows = pl.ds(pl.multiple_of((1 - c) * Z * ROWS, 16), Z * ROWS)
        wait_bytes(weights[j].at[rows, :], pair_r.at[j])

    for j in (1, 2, 0):
        ring_start(j)

    row = lax.broadcasted_iota(jnp.int32, (8, HD), 0)
    lane = lax.broadcasted_iota(jnp.int32, (8, HD), 1)
    stepped = lax.rem(row, 3)
    when = jnp.zeros((8, HD), F32)
    for s in range(STEPS):
        when = jnp.where(stepped == s, times[s].astype(F32), when)
    freq = jnp.exp(-math.log(10000.0) * lane.astype(F32) / HD)
    angle = 1000.0 * sigma(when) * freq
    emb = jnp.concatenate([jnp.cos(angle), jnp.sin(angle)], axis=1).astype(BF16)
    for load in loads:
        load.wait()
    mods = [lax.dot_general(emb, mw[j], NT, preferred_element_type=F32) for j in range(2)]
    row2 = lax.broadcasted_iota(jnp.int32, (8, 256), 0)
    mod_rows = jnp.where(row2 < 3, mods[0], mods[1])
    rows_here = xt[...].T
    for q in range(CHIPS):
        xs[q, 0:8] = rows_here[8 * q : 8 * q + 8]
        xs[q, 8:16] = mod_rows

    def x_copy(q, device):
        return remote(xs.at[q], xl.at[head], x_s, x_r, device)

    @pl.when(natural)
    def _():
        pltpu.make_async_copy(xs.at[me], xl.at[head], x_r).start()

    @pl.when(jnp.logical_not(natural))
    def _():
        x_copy(me, partner).start()

    def x_start(o, carry):
        yy, xx = chip_at(o)
        x_copy(yy * 4 + xx, dev(yy, xx, yl, z)).start()
        return carry

    lax.fori_loop(1, CHIPS, x_start, 0)

    def loop_hops(lo, hi):
        def body(k, carry):
            ring_hop(k)
            return carry

        lax.fori_loop(lo, hi, body, 0)

    loop_hops(1, 4)
    wait_bytes(xl, x_r)
    for k in range(8):
        a, b = xl[2 * k], xl[2 * k + 1]
        group = jnp.concatenate([a[:, :HD], a[:, HD:] + b[:, :HD], b[:, HD:]], axis=1)
        rows, cols = slice(8 * (k // 4), 8 * (k // 4) + 8), slice(384 * (k % 4), 384 * (k % 4) + 384)
        xp[rows, cols] = group[0:8]
        for i in range(6):
            modp[i, rows, cols] = jnp.broadcast_to(group[8 + i : 9 + i], (8, 384))

    def fold(sums):
        total = (sums[0:8] + sums[8:16]) * (1.0 / D)
        return jnp.concatenate([total, total], axis=0)

    def turn(i, d):
        return lax.rem(i + d, 4)

    def slot(yy, xx):
        return pl.ds(pl.multiple_of((yy * 4 + xx) * 16, 16), 16)

    def line(half, d):
        return dev(y, turn(x, d), c, z) if half == 0 else dev(turn(y, d), x, c, z)

    def origin(half, d):
        return slot(y, turn(x, 4 - d)) if half == 0 else slot(turn(y, 4 - d), x)

    def ag1(s, half, d, rows):
        block = hland.at[s, half, rows, :]
        return remote(block, block, ag_s, ag1_r.at[half, d - 1], line(half, d))

    def ag2(s, half, d, rows):
        block = hland.at[s, half, rows, :]
        return remote(block, block, ag_s, ag2_r.at[half], line(1 - half, d))

    def ag_start(s):
        rows = xp[...]
        delta = rows - fold(jnp.sum(rows, axis=1, keepdims=True))
        var = fold(jnp.sum(delta * delta, axis=1, keepdims=True))
        h = (delta * lax.rsqrt(var + 1e-06) * (1.0 + modp[s]) + modp[3 + s]).astype(BF16)
        mine = slot(y, x)
        for half in range(2):
            hland[s, half, mine, :] = h[:, half * PART : half * PART + PART]
        for d in (1, 3, 2):
            for half in range(2):
                ag1(s, half, d, mine).start()
        for d in (1, 3, 2):
            for half in range(2):
                ag2(s, half, d, mine).start()

    def ag_forward(s):
        for d in (1, 3, 2):
            for half in range(2):
                rows = origin(half, d)
                ag1(s, half, d, rows).wait_recv()
                for e in (1, 3, 2):
                    ag2(s, half, e, rows).start()

    def ag_end(s, half):
        wait_bytes(hland.at[s, half, 0:192, :], ag2_r.at[half])

    def ag_sent(s):
        wait_bytes(hland.at[s, :, 0:240, :], ag_s)

    def rs1(s, half, d):
        to = turn(y if half == 0 else x, d)
        block = tsend.at[half, pl.ds(pl.multiple_of(to * 64, 64), 64), :]
        return remote(
            block, r1.at[s, half, d - 1], rs1_s.at[half], rs1_r.at[half], line(1 - half, d)
        )

    def rs2(s, half, d):
        to = turn(x if half == 0 else y, d)
        block = p2.at[half, pl.ds(pl.multiple_of(to * 16, 16), 16), :]
        return remote(
            block, r2.at[s, half, d - 1], rs2_s.at[half], rs2_r.at[half], line(half, d)
        )

    def rs_middle(s):
        for half in range(2):
            here = pl.ds(pl.multiple_of((y if half == 0 else x) * 64, 64), 64)
            wait_bytes(r1.at[s, half], rs1_r.at[half])
            part = tsend[half, here, :].astype(F32)
            for d in range(3):
                part = part + r1[s, half, d].astype(F32)
            p2[half] = part.astype(BF16)
            for d in (1, 3, 2):
                rs2(s, half, d).start()

    def rs_sent():
        for half in range(2):
            wait_bytes(r1.at[0, half], rs1_s.at[half])
            wait_bytes(r2.at[0, half], rs2_s.at[half])

    def rs_end(s):
        parts = []
        for half in range(2):
            here = pl.ds(pl.multiple_of((x if half == 0 else y) * 16, 16), 16)
            wait_bytes(r2.at[s, half], rs2_r.at[half])
            part = p2[half, here, :].astype(F32)
            for d in (1, 3, 2):
                part = part + r2[s, half, d - 1].astype(F32)
            parts.append(part)
        return jnp.concatenate(parts, axis=1)

    def unpack(s, half):
        for m in range(8):
            block = hland[s, half, 32 * m : 32 * m + 32, :].astype(F32)
            rows = slice(16 * m, 16 * m + 16)
            low, high = half * PART, HALF + half * PART
            hb[rows, low : low + PART] = jnp.concatenate([block[0:8], block[16:24]], axis=0).astype(BF16)
            hb[rows, high : high + PART] = jnp.concatenate([block[8:16], block[24:32]], axis=0).astype(BF16)

    ag_start(0)
    loop_hops(4, 5)
    ag_forward(0)
    loop_hops(5, 7)
    for half in range(2):
        ag_end(0, half)
        unpack(0, half)
    ring_hop(7, last=True)
    ring_end(0)
    ring_end(1)
    pair_all(0)

    wait_bytes(kv.at[0], cache_r.at[0])
    wait_bytes(gains, cache_r.at[1])

    def kv_block(s, cc, zz, part=None):
        start, size = (cc * Z + zz) * TOK, TOK
        if part is not None:
            start, size = start + part * (TOK // 2), TOK // 2
        return kv.at[s + 1, :, pl.ds(pl.multiple_of(start, 16), size), :]

    def kring_copy(s, d, k, far, zz, part=None):
        block = kv_block(s, c, zz, part)
        device = z_far[d] if far else z_next[d]
        return remote(block, block, kring_s.at[s, min(k, 1)], kring_r.at[s, d, k, far], device)

    def kpair_copy(s, zz, rest=1):
        block = kv_block(s, c, zz)
        return remote(block, block, kring_s.at[s, rest], kpair_r.at[s], partner)

    def kv_send(s, k):
        for d in range(2):
            kring_copy(s, d, k, 1, source(d, 2 * k), d if k == 3 else None).start()
        for d in range(2):
            kring_copy(s, d, k, 0, source(d, 2 * k)).start()

    def kv_start(s):
        kv_send(s, 0)
        kpair_copy(s, z, 0).start()

    def kv_stage(s, k):
        for d in range(2):
            kring_copy(s, d, k - 1, 1, source(d, 2 * k), d if k == 4 else None).wait_recv()
        if k < 4:
            kv_send(s, k)
            for d in range(2):
                kpair_copy(s, source(d, 2 * k)).start()
        else:
            kpair_copy(s, source(0, 8)).start()
        for d in range(2):
            zz = source(d, 2 * k - 1)
            kring_copy(s, d, k - 1, 0, zz).wait_recv()
            kpair_copy(s, zz).start()

    def kv_wait(s):
        rows = pl.ds(pl.multiple_of((1 - c) * Z * TOK, 16), Z * TOK)
        wait_bytes(kv.at[s + 1, :, rows, :], kpair_r.at[s])

    def kv_sent_own(s):
        wait_bytes(kv.at[s + 1, :, 0 : 5 * TOK, :], kring_s.at[s, 0])

    def kv_sent_rest(s):
        wait_bytes(kv.at[s + 1, :, 0 : 26 * TOK, :], kring_s.at[s, 1])

    def rms(values, gain):
        return values * lax.rsqrt(jnp.mean(values * values, axis=1, keepdims=True) + 1e-06) * gain

    def f_copy(r):
        rows = pl.ds(pl.multiple_of(me * 8, 8), 8)
        return remote(fs.at[r], fl.at[rows, :], f_s, f_r, (c * Z + z, r))

    def f_self():
        rows = pl.ds(pl.multiple_of(me * 8, 8), 8)
        return pltpu.make_async_copy(fs.at[head], fl.at[rows, :], f_r)

    def f_start():
        for r in range(CHIPS):
            k = r // 2
            first = 384 * (k % 4) + HD * (r % 2)
            fs[r] = xp[8 * (k // 4) : 8 * (k // 4) + 8, first : first + 256]

        def body(o, carry):
            f_copy(lax.rem(head + o, CHIPS)).start()
            return carry

        lax.fori_loop(1, CHIPS, body, 0)

        @pl.when(natural)
        def _():
            f_self().start()

        @pl.when(jnp.logical_not(natural))
        def _():
            f_copy(head).start()

    def f_wait():
        wait_bytes(fl, f_r)
        xt[...] = fl[...].T

    def t_copy(r):
        return remote(tt.at[r], ft.at[me], t_s, t_r, (c * Z + z, r))

    own_rows = pl.ds(pl.multiple_of(own * TOK, 16), TOK)

    for s in range(STEPS):
        qkv = jnp.dot(hb[...], wq[...], preferred_element_type=F32)
        query = rms(qkv[:, 0:HD], gains[0]).astype(BF16)
        fresh = (rms(qkv[:, HD : 2 * HD], gains[1]).astype(BF16), qkv[:, 2 * HD :].astype(BF16))
        if s > 0:
            kv_sent_own(s - 1)
        for i in range(2):
            old = kv[s, i, own_rows, :].astype(F32)
            if s < STEPS - 1:
                change = (fresh[i].astype(F32) - old).astype(BF16)
                kv[s + 1, i, own_rows, :] = (old + change.astype(F32)).astype(BF16)
            kv[s, i, own_rows, :] = fresh[i]
        if s < STEPS - 1:
            kv_start(s)
        if s == 0:
            pair_all(1)
        og[:, HD:512] = jax.nn.gelu(
            jnp.dot(hb[...], wi[...], preferred_element_type=F32), approximate=True
        ).astype(BF16)
        if s == 0:
            ring_end(2)
        else:
            kv_stage(s - 1, 4)
            kv_wait(s - 1)
        top = jnp.full((TOK, 1), -jnp.inf, F32)
        for j in range(KEYS // CHUNK):
            cols = slice(CHUNK * j, CHUNK * j + CHUNK)
            score = lax.dot_general(query, kv[s, 0, cols, :], NT, preferred_element_type=F32)
            score = score * (1.0 / math.sqrt(HD))
            scores[:, cols] = score
            top = jnp.maximum(top, jnp.max(score, axis=1, keepdims=True))
        mass = jnp.zeros((TOK, 1), F32)
        mixed = jnp.zeros((TOK, HD), F32)
        for j in range(KEYS // CHUNK):
            cols = slice(CHUNK * j, CHUNK * j + CHUNK)
            weight = jnp.exp(scores[:, cols] - top)
            mass = mass + jnp.sum(weight, axis=1, keepdims=True)
            mixed = mixed + jnp.dot(weight.astype(BF16), kv[s, 1, cols, :], preferred_element_type=F32)
        og[:, 0:HD] = (mixed / mass).astype(BF16)
        if s == 0:
            pair_all(2)
        elif s < STEPS - 1:
            rs_sent()
        level = [sigma(jnp.full((16, HD), times[s + i].astype(F32))) for i in range(2)]
        gap = (level[1] - level[0])[:, 0:1]
        if s == STEPS - 1:
            break
        for n in range(4):
            half, first = n // 2, 384 * (n % 2)
            cols = slice(384 * n, 384 * n + 384)
            upper = slice(HALF + 384 * n, HALF + 384 * n + 384)
            low = lax.dot_general(og[...], wo[cols, :], NT, preferred_element_type=F32)
            high = lax.dot_general(og[...], wo[upper, :], NT, preferred_element_type=F32)
            for q in range(CHIPS):
                rows = slice(8 * q, 8 * q + 8)
                spot = 16 * (q if half == 0 else 4 * (q % 4) + q // 4)
                both = jnp.concatenate([low[rows], high[rows]], axis=0).astype(BF16)
                tsend[half, spot : spot + 16, first : first + 384] = both
            if n % 2 == 1:
                for d in (1, 3, 2):
                    rs1(s, half, d).start()
        kv_stage(s, 1)
        rs_middle(s)
        kv_stage(s, 2)
        xp[...] = xp[...] + gap * rs_end(s)
        ag_sent(s)
        ag_start(s + 1)
        kv_stage(s, 3)
        ag_forward(s + 1)
        if s == STEPS - 2:
            f_start()
        for half in range(2):
            ag_end(s + 1, half)
            unpack(s + 1, half)

    for g in range(4):
        group = lax.rem(lax.div(head, 4) + g, 4)
        features = pl.ds(pl.multiple_of(group * 768, 16), 768)
        term = lax.dot_general(wo[features, :], og[...], NT, preferred_element_type=F32).astype(BF16)
        for i in range(4):
            r = group * 4 + i
            tt[r] = term[192 * i : 192 * i + 192]

            @pl.when(jnp.logical_and(natural, r == head))
            def _():
                pltpu.make_async_copy(tt.at[r], ft.at[me], t_r).start()

            @pl.when(jnp.logical_not(jnp.logical_and(natural, r == head)))
            def _():
                t_copy(r).start()

    f_wait()
    wait_bytes(ft, t_r)
    total = jnp.zeros((192, TOK), F32)
    for q in range(CHIPS):
        total = total + ft[q].astype(F32)
    out[...] = xt[place, :] + gap[0:1, 0:1] * total

    rs_sent()
    ag_sent(STEPS - 1)
    for s in range(STEPS - 1):
        kv_sent_rest(s)
    for j in range(3):
        wait_bytes(weights[j].at[0 : Z * ROWS, :], pair_s.at[j])
        wait_bytes(weights[j].at[0 : (15 if j > 0 else 13) * ROWS, :], ring_s.at[j])
    wait_bytes(wq.at[0 : 2 * ROWS, :], first_s)

    @pl.when(natural)
    def _():
        wait_bytes(xs.at[0:15], x_s)
        wait_bytes(fs.at[0:15], f_s)
        wait_bytes(tt.at[0:15], t_s)
        wait_bytes(kv.at[0], cache_s.at[0])
        wait_bytes(gains, cache_s.at[1])

    @pl.when(jnp.logical_not(natural))
    def _():
        wait_bytes(xs, x_s)
        wait_bytes(fs, f_s)
        wait_bytes(tt, t_s)
        wait_bytes(wo.at[0:240, :], swap_s)


def on_device(
    state, mod_weight, w_qkv, q_gain, k_gain, w_in, w_attn, w_out, cache_keys, cache_values, timesteps
):
    vmem = pl.BlockSpec(memory_space=pltpu.VMEM)
    hbm = pl.BlockSpec(memory_space=pl.ANY)
    smem = pl.BlockSpec(memory_space=pltpu.SMEM)
    dma = pltpu.SemaphoreType.DMA
    one = pltpu.SemaphoreType.DMA
    result = pl.pallas_call(
        kernel,
        out_shape=jax.ShapeDtypeStruct((192, TOK), F32),
        in_specs=[smem, hbm, hbm, hbm, hbm, hbm, hbm, hbm, hbm, hbm, hbm],
        out_specs=vmem,
        scratch_shapes=[
            pltpu.VMEM((D, 384), BF16),
            pltpu.VMEM((D, 384), BF16),
            pltpu.VMEM((D, 512), BF16),
            pltpu.VMEM((STEPS, 2, KEYS, HD), BF16),
            pltpu.VMEM((STEPS, 2, CHIPS * 16, PART), BF16),
            pltpu.VMEM((STEPS, 2, 3, 64, PART), BF16),
            pltpu.VMEM((STEPS, 2, 3, 16, PART), BF16),
            pltpu.VMEM((2, CHIPS * 16, PART), BF16),
            pltpu.VMEM((2, 64, PART), BF16),
            pltpu.VMEM((TOK, D), BF16),
            pltpu.VMEM((TOK, 512), BF16),
            pltpu.VMEM((TOK, KEYS), F32),
            pltpu.VMEM((CHIPS, 16, 256), F32),
            pltpu.VMEM((CHIPS, 16, 256), F32),
            pltpu.VMEM((CHIPS, 8, 256), F32),
            pltpu.VMEM((TOK, 256), F32),
            pltpu.VMEM((CHIPS, 192, TOK), BF16),
            pltpu.VMEM((CHIPS, 192, TOK), BF16),
            pltpu.VMEM((256, TOK), F32),
            pltpu.VMEM((2, 256, 256), BF16),
            pltpu.VMEM((6, 16, HALF), F32),
            pltpu.VMEM((16, HALF), F32),
            pltpu.VMEM((2, 1, HD), F32),
            dma((2,)), dma((2,)), one, dma((3,)), one, dma((3,)), dma((3, 2, 2)), dma((3,)), dma((3,)),
            dma((2, 2)), dma((2, 2, 4, 2)), dma((2,)), one, one, one, dma((2, 3)), dma((2,)),
            dma((2,)), dma((2,)), dma((2,)), dma((2,)), one, one, one, one, dma((2,)),
        ],
        compiler_params=pltpu.CompilerParams(
            collective_id=0, has_side_effects=True, vmem_limit_bytes=60 * 1024 * 1024
        ),
    )(
        timesteps,
        state.T,
        jnp.transpose(mod_weight, (1, 2, 0)),
        w_qkv.reshape(ROWS, 384),
        w_in,
        w_attn.T,
        w_out.T,
        q_gain,
        k_gain,
        cache_keys.reshape(KEYS, HD),
        cache_values.reshape(KEYS, HD),
    )
    return result.T


def solution(mesh):
    in_specs = (
        P("patch", "head"),
        P(None, None, "head"),
        P("patch", "head", None),
        P("head", None),
        P("head", None),
        P("patch", "head"),
        P("head", "patch"),
        P("head", "patch"),
        P(None, "head", None),
        P(None, "head", None),
        P(),
    )
    return jax.shard_map(
        on_device, mesh=mesh, in_specs=in_specs, out_specs=P("patch", "head"), check_vma=False
    )
```

time: 138 us -> 129 us (0.935)
  Pallas kernels: 137 us -> 127 us
    pallas_call x1, Pallas kernels: 137 us -> 127 us  [on_device(): pl.pallas_call(kernel, out_shape=jax.ShapeDtypeStruct((192, TOK), F32), i...]
where the time goes in v3:
time: 129 us; the launch traced here: 128 us
  Pallas kernels  127 us (98%)
  local copies, waits for them, and re-layouts  1.54 us (1%)
    pallas_call x1, Pallas kernels, on_device(): pl.pallas_call(kernel, out_shape=jax.ShapeDtypeStruct((192, TOK), F32), i...  127 us

profile of v3, /device:TPU:1, one launch (start us, length us, event | category | flops | bytes accessed | tf_op | source)
XLA Modules:
  0.0 128.4 jit_solution(2333627076535796804)
XLA Ops:
  0.0 126.8 %shard_map.109 = f32[192,128]{1,0:T(8,128)} custom-call(s32[4]{0:T(128)} %times.1, f32[192,128]{1,0:T(8,128)} %bitcast.12, bf16[2,192,256]{2,1,0:T(8,128)(2,1)} %bitcast.11, bf16[96,384]{1,0:T(8,128)(2,1)} %bitcast.13, bf16[96,384]{1,0:T(8,128)(2,1)} %w_in.1, bf16[96,128]{1,0:T(8,128)(2,1)} %bitcast.15, bf16[96,384]{1,0:T(8,128)(2,1)} %bitcast.14, ...), custom_call_target="tpu_custom_call" | custom-call | tf_op jit(solution)/shard_map/pallas_call | solution.py:573
  126.8 1.5 %copy.13 = f32[128,192]{0,1:T(8,128)} copy(f32[128,192]{0,1:T(8,128)} %bitcast.10) | data formatting | bytes 196608

commit v4 on v3

--- a/solution.py
+++ b/solution.py
@@ -119,9 +119,11 @@
 
     pl.semaphore_wait(barrier, 37)
 
-    for d in range(2):
-        src, dst = shard(0, patch)
-        remote(src, dst, first_s, ring_r.at[0, d, 0], twin_next[d]).start()
+    for half in range(2):
+        for d in range(2):
+            src = w_qkv.at[half * (ROWS // 2) : (half + 1) * (ROWS // 2), :]
+            rows = pl.ds(pl.multiple_of(patch * ROWS + half * (ROWS // 2), 16), ROWS // 2)
+            remote(src, wq.at[rows, :], first_s, ring_r.at[0, half, d, 0], twin_next[d]).start()
     part_of = (0, 1, 2, 2)
 
     @pl.when(natural)
@@ -143,9 +145,9 @@
         part = slab(j, zz)
         return remote(part, part, pair_s.at[j], pair_r.at[j], partner)
 
-    def ring_copy(j, d, k, zz, half=None):
+    def ring_copy(j, half, d, k, zz):
         block = slab(j, zz, half)
-        return remote(block, block, ring_s.at[j], ring_r.at[j, d, lax.rem(k, 2)], z_next[d])
+        return remote(block, block, ring_s.at[j], ring_r.at[j, half, d, lax.rem(k, 2)], z_next[d])
 
     def source(d, k):
         return lax.rem(z + Z - k, Z) if d == 0 else lax.rem(z + k, Z)
@@ -153,23 +155,25 @@
     def ring_start(j):
         wait_bytes(slab(j, z), swap_r.at[j])
         if j > 0:
+            for half in range(2):
+                for d in range(2):
+                    ring_copy(j, half, d, 0, z).start()
+        pair_copy(j, z).start()
+
+    def ring_hop(j, k, last=False):
+        for half in range(2):
             for d in range(2):
-                ring_copy(j, d, 0, z).start()
-        pair_copy(j, z).start()
-
-    def ring_hop(k, last=False):
-        for j in range(3):
+                ring_copy(j, half, d, k - 1, source(d, k)).wait_recv()
             for d in range(2):
-                ring_copy(j, d, k - 1, source(d, k)).wait_recv()
-            for d in range(2):
-                ring_copy(j, d, k, source(d, k), d if last else None).start()
-            for d in range(2):
-                pair_copy(j, source(d, k)).start()
+                if not last or half == d:
+                    ring_copy(j, half, d, k, source(d, k)).start()
+        for d in range(2):
+            pair_copy(j, source(d, k)).start()
 
     def ring_end(j):
         zz = source(0, 8)
         for d in range(2):
-            ring_copy(j, d, 7, zz, d).wait_recv()
+            ring_copy(j, d, d, 7, zz).wait_recv()
         pair_copy(j, zz).start()
 
     def pair_all(j):
@@ -216,14 +220,16 @@
 
     lax.fori_loop(1, CHIPS, x_start, 0)
 
-    def loop_hops(lo, hi):
-        def body(k, carry):
-            ring_hop(k)
-            return carry
-
-        lax.fori_loop(lo, hi, body, 0)
-
-    loop_hops(1, 4)
+    def hop(k, carry):
+        ring_hop(0, k)
+        ring_hop(1, k)
+        ring_hop(2, k)
+        return carry
+
+    ring_hop(0, 1)
+    ring_hop(1, 1)
+    ring_hop(2, 1)
+    lax.fori_loop(2, 4, hop, 0)
     wait_bytes(xl, x_r)
     for k in range(8):
         a, b = xl[2 * k], xl[2 * k + 1]
@@ -336,13 +342,15 @@
             hb[rows, high : high + PART] = jnp.concatenate([block[8:16], block[24:32]], axis=0).astype(BF16)
 
     ag_start(0)
-    loop_hops(4, 5)
+    lax.fori_loop(4, 5, hop, 0)
     ag_forward(0)
-    loop_hops(5, 7)
+    lax.fori_loop(5, 7, hop, 0)
     for half in range(2):
         ag_end(0, half)
         unpack(0, half)
-    ring_hop(7, last=True)
+    ring_hop(0, 7, last=True)
+    ring_hop(1, 7, last=True)
+    ring_hop(2, 7, last=True)
     ring_end(0)
     ring_end(1)
     pair_all(0)
@@ -384,10 +392,11 @@
                 kpair_copy(s, source(d, 2 * k)).start()
         else:
             kpair_copy(s, source(0, 8)).start()
-        for d in range(2):
-            zz = source(d, 2 * k - 1)
-            kring_copy(s, d, k - 1, 0, zz).wait_recv()
-            kpair_copy(s, zz).start()
+        for near in (k - 1,):
+            for d in range(2):
+                zz = source(d, 2 * near + 1)
+                kring_copy(s, d, near, 0, zz).wait_recv()
+                kpair_copy(s, zz).start()
 
     def kv_wait(s):
         rows = pl.ds(pl.multiple_of((1 - c) * Z * TOK, 16), Z * TOK)
@@ -599,7 +608,7 @@
             pltpu.VMEM((6, 16, HALF), F32),
             pltpu.VMEM((16, HALF), F32),
             pltpu.VMEM((2, 1, HD), F32),
-            dma((2,)), dma((2,)), one, dma((3,)), one, dma((3,)), dma((3, 2, 2)), dma((3,)), dma((3,)),
+            dma((2,)), dma((2,)), one, dma((3,)), one, dma((3,)), dma((3, 2, 2, 2)), dma((3,)), dma((3,)),
             dma((2, 2)), dma((2, 2, 4, 2)), dma((2,)), one, one, one, dma((2, 3)), dma((2,)),
             dma((2,)), dma((2,)), dma((2,)), dma((2,)), one, one, one, one, dma((2,)),
         ],

time: 129 us -> 126 us (0.977)
  Pallas kernels: 127 us -> 125 us
    pallas_call x1, Pallas kernels: 127 us -> 125 us  [on_device(): pl.pallas_call(kernel, out_shape=jax.ShapeDtypeStruct((192, TOK), F32), i...]
where the time goes in v4:
time: 126 us
  Pallas kernels  125 us (99%)
  local copies, waits for them, and re-layouts  1.54 us (1%)
    pallas_call x1, Pallas kernels, on_device(): pl.pallas_call(kernel, out_shape=jax.ShapeDtypeStruct((192, TOK), F32), i...  125 us

profile of v4, /device:TPU:1, one launch (start us, length us, event | category | flops | bytes accessed | tf_op | source)
XLA Modules:
  0.0 126.1 jit_solution(4638224026659820572)
XLA Ops:
  0.0 124.6 %shard_map.109 = f32[192,128]{1,0:T(8,128)} custom-call(s32[4]{0:T(128)} %times.1, f32[192,128]{1,0:T(8,128)} %bitcast.12, bf16[2,192,256]{2,1,0:T(8,128)(2,1)} %bitcast.11, bf16[96,384]{1,0:T(8,128)(2,1)} %bitcast.13, bf16[96,384]{1,0:T(8,128)(2,1)} %w_in.1, bf16[96,128]{1,0:T(8,128)(2,1)} %bitcast.15, bf16[96,384]{1,0:T(8,128)(2,1)} %bitcast.14, ...), custom_call_target="tpu_custom_call" | custom-call | tf_op jit(solution)/shard_map/pallas_call | solution.py:582
  124.6 1.5 %copy.13 = f32[128,192]{0,1:T(8,128)} copy(f32[128,192]{0,1:T(8,128)} %bitcast.10) | data formatting | bytes 196608

commit v5 on v4

--- a/solution.py
+++ b/solution.py
@@ -21,7 +21,7 @@
 HD = 128
 ROWS = 96
 KEYS = 4096
-CHUNK = 512
+CHUNK = 1024
 NT = (((1,), (1,)), ((), ()))
 
 
@@ -449,9 +449,8 @@
     own_rows = pl.ds(pl.multiple_of(own * TOK, 16), TOK)
 
     for s in range(STEPS):
-        qkv = jnp.dot(hb[...], wq[...], preferred_element_type=F32)
-        query = rms(qkv[:, 0:HD], gains[0]).astype(BF16)
-        fresh = (rms(qkv[:, HD : 2 * HD], gains[1]).astype(BF16), qkv[:, 2 * HD :].astype(BF16))
+        both = jnp.dot(hb[...], wq[:, HD:384], preferred_element_type=F32)
+        fresh = (rms(both[:, :HD], gains[1]).astype(BF16), both[:, HD:].astype(BF16))
         if s > 0:
             kv_sent_own(s - 1)
         for i in range(2):
@@ -462,6 +461,7 @@
             kv[s, i, own_rows, :] = fresh[i]
         if s < STEPS - 1:
             kv_start(s)
+        query = rms(jnp.dot(hb[...], wq[:, 0:HD], preferred_element_type=F32), gains[0]).astype(BF16)
         if s == 0:
             pair_all(1)
         og[:, HD:512] = jax.nn.gelu(
@@ -476,14 +476,13 @@
         for j in range(KEYS // CHUNK):
             cols = slice(CHUNK * j, CHUNK * j + CHUNK)
             score = lax.dot_general(query, kv[s, 0, cols, :], NT, preferred_element_type=F32)
-            score = score * (1.0 / math.sqrt(HD))
             scores[:, cols] = score
             top = jnp.maximum(top, jnp.max(score, axis=1, keepdims=True))
         mass = jnp.zeros((TOK, 1), F32)
         mixed = jnp.zeros((TOK, HD), F32)
         for j in range(KEYS // CHUNK):
             cols = slice(CHUNK * j, CHUNK * j + CHUNK)
-            weight = jnp.exp(scores[:, cols] - top)
+            weight = jnp.exp2((scores[:, cols] - top) * (math.log2(math.e) / math.sqrt(HD)))
             mass = mass + jnp.sum(weight, axis=1, keepdims=True)
             mixed = mixed + jnp.dot(weight.astype(BF16), kv[s, 1, cols, :], preferred_element_type=F32)
         og[:, 0:HD] = (mixed / mass).astype(BF16)
@@ -495,20 +494,18 @@
         gap = (level[1] - level[0])[:, 0:1]
         if s == STEPS - 1:
             break
-        for n in range(4):
-            half, first = n // 2, 384 * (n % 2)
-            cols = slice(384 * n, 384 * n + 384)
-            upper = slice(HALF + 384 * n, HALF + 384 * n + 384)
+        for half in range(2):
+            cols = slice(PART * half, PART * half + PART)
+            upper = slice(HALF + PART * half, HALF + PART * half + PART)
             low = lax.dot_general(og[...], wo[cols, :], NT, preferred_element_type=F32)
             high = lax.dot_general(og[...], wo[upper, :], NT, preferred_element_type=F32)
             for q in range(CHIPS):
                 rows = slice(8 * q, 8 * q + 8)
                 spot = 16 * (q if half == 0 else 4 * (q % 4) + q // 4)
                 both = jnp.concatenate([low[rows], high[rows]], axis=0).astype(BF16)
-                tsend[half, spot : spot + 16, first : first + 384] = both
-            if n % 2 == 1:
-                for d in (1, 3, 2):
-                    rs1(s, half, d).start()
+                tsend[half, spot : spot + 16, :] = both
+            for d in (1, 3, 2):
+                rs1(s, half, d).start()
         kv_stage(s, 1)
         rs_middle(s)
         kv_stage(s, 2)

time: 126 us -> 127 us (level)
  no operation moved by 1% of the time
where the time goes in v5:
time: 127 us
  Pallas kernels  126 us (99%)
  local copies, waits for them, and re-layouts  1.54 us (1%)
    pallas_call x1, Pallas kernels, on_device(): pl.pallas_call(kernel, out_shape=jax.ShapeDtypeStruct((192, TOK), F32), i...  126 us

profile of v5, /device:TPU:1, one launch (start us, length us, event | category | flops | bytes accessed | tf_op | source)
XLA Modules:
  0.0 127.1 jit_solution(6822851021140054199)
XLA Ops:
  0.0 125.6 %shard_map.109 = f32[192,128]{1,0:T(8,128)} custom-call(s32[4]{0:T(128)} %times.1, f32[192,128]{1,0:T(8,128)} %bitcast.12, bf16[2,192,256]{2,1,0:T(8,128)(2,1)} %bitcast.11, bf16[96,384]{1,0:T(8,128)(2,1)} %bitcast.13, bf16[96,384]{1,0:T(8,128)(2,1)} %w_in.1, bf16[96,128]{1,0:T(8,128)(2,1)} %bitcast.15, bf16[96,384]{1,0:T(8,128)(2,1)} %bitcast.14, ...), custom_call_target="tpu_custom_call" | custom-call | tf_op jit(solution)/shard_map/pallas_call | solution.py:579
  125.6 1.5 %copy.13 = f32[128,192]{0,1:T(8,128)} copy(f32[128,192]{0,1:T(8,128)} %bitcast.10) | data formatting | bytes 196608
